TPU v7x, 128 devices: a whole 4x4x4 slice. The times are simulated.
128 devices in a mesh: gx: 16 (over x_lo, y, core), gy: 8 (over z, x_hi).
Axes of the slice: x: 4 (x_hi: 2, x_lo: 2; x = x_hi * 2 + x_lo), y: 4, z: 4, core: 2. Of those that a mesh axis runs over, the one named last changes fastest.
Arguments:
- segment_wattage_table: float32 [524288, 128], P(('gx', 'gy')), may hold values from 0.05 to 2
- segment_target_tile: int32 [524288], P(('gx', 'gy')), may hold values from 0 to 127, as said below
- occupied_slot_tally: int32 [128], P(('gx', 'gy')), may hold values from 2048 to 4096, as said below
- segment_tile_position: int32 [524288], P(('gx', 'gy')), may hold values from 0 to 4095
- stratum_substance: int32 [8], replicated, may hold values from 0 to 3, as said below
- substance_transport_base: float32 [4], replicated, may hold values from 0.5 to 4
- substance_thermal_slope: float32 [4], replicated, may hold values from 0.2 to 1
- thermal_scaling_factor: float32 [8, 4096, 2048], P(None, 'gx', 'gy'), may hold values from 0.5 to 2
- starting_warmth_excess: float32 [8, 4096, 2048], P(None, 'gx', 'gy'), may hold values from 0.5 to 1.5
Outputs:
- site_wattage_field: float32 [8, 4096, 2048], P(None, 'gx', 'gy')
- final_warmth_field: float32 [8, 4096, 2048], P(None, 'gx', 'gy')
Inputs may be any that keep to these rules, and one draw needn't show every extreme that they name: `segment_target_tile`: among the rows of one owner at most 48 name the same tile; one tile is named by exactly 48 live rows of every owner. `occupied_slot_tally`: some owner has all 4096 slots live. `stratum_substance`: every material is used by some layer.
All inputs are finite; a program needn't handle non-finite values.
Results may differ from a plain program's by a relative error of at most 0.0003.
Values sent between devices are 32-bit elements; how exact they have to be, the bound alone decides.
No kernel may reach another device: no remote copies, remote signals or barrier semaphores. Data moves between devices by JAX's collectives and lax.ppermute only.
A program may use at most 128 MiB of HBM per device.

v0:
```python
import jax
import jax.numpy as jnp
from jax import lax
from jax.experimental import pallas as pl
from jax.experimental.pallas import tpu as pltpu
from jax.sharding import PartitionSpec as P

RUN = 128
SWEEPS = 3
CAP = 48
CHUNK = CAP + 1
LAYERS = 8
NX = 256
NY = 256
GROUPS = NX // 8
POSITIONS = LAYERS * NX * NY // RUN
ACCS = 4
WALL = 1e30
BASE = 16
ROWS = 280
VMEM_LIMIT = 60 * 1024 * 1024
F32 = jnp.float32
BF16 = jnp.bfloat16


def iota(shape, dim):
    return lax.broadcasted_iota(jnp.int32, shape, dim)


def pack_kernel(tally_ref, target_ref, place_ref, table_ref, out_ref, dest_v, dest_s, sem):
    tally = tally_ref[0]
    tiles = 128
    sub = iota((tiles, RUN), 0)
    lane = iota((1, RUN), 1)
    tri_row = iota((RUN, 2 * RUN), 0)
    tri_col = iota((RUN, 2 * RUN), 1)
    tri = jnp.where((tri_row <= tri_col) | (tri_col >= RUN), 1.0, 0.0).astype(BF16)

    def rank_group(g, carry):
        seen, placed = carry
        live = (lane + g * RUN) < tally
        tgt = target_ref[pl.ds(g, 1), :]
        match = sub == jnp.where(live, tgt, -1)
        onehot = jnp.where(match, 1.0, 0.0)
        run = jnp.dot(onehot.astype(BF16), tri, preferred_element_type=F32)
        rank = jnp.sum(jnp.where(match, seen + run[:, :RUN], 0.0), axis=0, keepdims=True)
        rank = rank.astype(jnp.int32) - 1
        dest_v[pl.ds(g, 1), :] = jnp.where(live, tgt * CHUNK + rank, CAP)
        spot = place_ref[pl.ds(g, 1), :]
        spot = (spot & ~15) | ((spot & 1) << 3) | ((spot >> 1) & 7)
        spot = spot + 1
        digits = jnp.where(sub < 64, spot & 63, spot >> 6)
        chosen = jnp.where((sub & 63) == rank, digits, 0).astype(F32)
        placed = placed + lax.dot_general(
            onehot.astype(BF16),
            chosen.astype(BF16),
            (((1,), (1,)), ((), ())),
            preferred_element_type=F32,
        )
        return seen + run[:, RUN:], placed

    zero = jnp.zeros((tiles, RUN), F32)
    seen, placed = lax.fori_loop(0, target_ref.shape[0], rank_group, (zero, zero))
    placed = placed + 64.0 * pltpu.roll(placed, 64, 1)
    copy = pltpu.make_async_copy(dest_v, dest_s, sem)
    copy.start()
    copy.wait()

    def move(j, _):
        for k in range(16):
            row = j * 16 + k
            d = dest_s[j // 8, (j % 8) * 16 + k]
            out_ref[pl.ds(d, 1), :] = table_ref[pl.ds(row, 1), :]
        return 0

    lax.fori_loop(0, (tally + 15) // 16, move, 0)
    for t in range(tiles):
        out_ref[t * CHUNK + CAP : t * CHUNK + CAP + 1, :] = placed[t : t + 1, :]


def pack(tally, target, place, table):
    tiles = 128
    return pl.pallas_call(
        pack_kernel,
        out_shape=jax.ShapeDtypeStruct((tiles * CHUNK, RUN), F32),
        in_specs=[
            pl.BlockSpec(memory_space=pltpu.SMEM),
            pl.BlockSpec(memory_space=pltpu.VMEM),
            pl.BlockSpec(memory_space=pltpu.VMEM),
            pl.BlockSpec(memory_space=pltpu.VMEM),
        ],
        out_specs=pl.BlockSpec(memory_space=pltpu.VMEM),
        scratch_shapes=[
            pltpu.VMEM((32, RUN), jnp.int32),
            pltpu.SMEM((32, RUN), jnp.int32),
            pltpu.SemaphoreType.DMA,
        ],
        compiler_params=pltpu.CompilerParams(vmem_limit_bytes=VMEM_LIMIT),
    )(tally, target, place, table)


def fold_left(kept, value, g, slot):
    return jnp.where(slot == g, pltpu.roll(value, (4 * g) % RUN, 1), kept)


def fold_right(kept, value, g, slot):
    return jnp.where(slot == g, pltpu.roll(value, (4 * g + 4) % RUN, 1), kept)


def prepare_kernel(
    kind_ref, base_ref, warmth_ref, scale_ref, q_ref, left_ref, right_ref, low_ref, high_ref
):
    slot = iota((8, RUN), 1) // 4

    def layer(l, _):
        inverse = 1.0 / jnp.full((8, RUN), base_ref[kind_ref[l]], F32)
        sides = [jnp.zeros((8, RUN), F32) for _ in range(4)]
        for g in range(GROUPS):
            for h in range(2):
                cols = slice(h * RUN, (h + 1) * RUN)
                t = warmth_ref[l, 8 * g : 8 * g + 8, cols]
                q = inverse / scale_ref[l, 8 * g : 8 * g + 8, cols]
                q_ref[l, 8 * g : 8 * g + 8, cols] = q
                if h == 0:
                    sides[0] = fold_left(sides[0], t, g, slot)
                    sides[1] = fold_left(sides[1], q, g, slot)
                else:
                    sides[2] = fold_right(sides[2], t, g, slot)
                    sides[3] = fold_right(sides[3], q, g, slot)
                if g == 0:
                    low_ref[0, l, :, cols] = t[:4]
                    low_ref[1, l, :, cols] = q[:4]
                if g == GROUPS - 1:
                    high_ref[0, l, :, cols] = t[4:]
                    high_ref[1, l, :, cols] = q[4:]
        left_ref[0, l] = sides[0]
        left_ref[1, l] = sides[1]
        right_ref[0, l] = sides[2]
        right_ref[1, l] = sides[3]
        return 0

    lax.fori_loop(0, LAYERS, layer, 0)


def prepare(kind, base, warmth, scale):
    vmem = pl.BlockSpec(memory_space=pltpu.VMEM)
    smem = pl.BlockSpec(memory_space=pltpu.SMEM)
    return pl.pallas_call(
        prepare_kernel,
        out_shape=(
            jax.ShapeDtypeStruct(warmth.shape, F32),
            jax.ShapeDtypeStruct((2, LAYERS, 8, RUN), F32),
            jax.ShapeDtypeStruct((2, LAYERS, 8, RUN), F32),
            jax.ShapeDtypeStruct((2, LAYERS, 4, NY), F32),
            jax.ShapeDtypeStruct((2, LAYERS, 4, NY), F32),
        ),
        in_specs=[smem, smem, vmem, vmem],
        out_specs=(vmem,) * 5,
        compiler_params=pltpu.CompilerParams(vmem_limit_bytes=VMEM_LIMIT),
        cost_estimate=pl.CostEstimate(flops=8000000, bytes_accessed=6300000, transcendentals=0),
    )(kind, base, warmth, scale)


def gather_kernel(
    inc_ref, left_in, right_in, low_in, high_in,
    field_ref, left_ref, right_ref, low_ref, high_ref,
    acc0, acc1, acc2, acc3, spot_v, spot_s, sem,
):
    accs = (acc0, acc1, acc2, acc3)
    tiles = 128
    for t in range(tiles):
        row = inc_ref[t * CHUNK + CAP : t * CHUNK + CAP + 1, :]
        spot_v[t : t + 1, :] = jnp.where(row > 0.5, row.astype(jnp.int32) - 1, POSITIONS)
    copy = pltpu.make_async_copy(spot_v, spot_s, sem)
    copy.start()

    def clear(i, _):
        for acc in accs:
            acc[pl.ds(pl.multiple_of(i * 64, 64), 64), :] = jnp.zeros((64, RUN), F32)
        return 0

    lax.fori_loop(0, POSITIONS // 64, clear, 0)
    copy.wait()

    def source(s, _):
        for p in range(CAP):
            o = spot_s[s, p]
            acc = accs[p % ACCS]
            acc[pl.ds(o, 1), :] += inc_ref[pl.ds(s * CHUNK + p, 1), :]
        return 0

    lax.fori_loop(0, tiles, source, 0)
    left_ref[0:2] = left_in[...]
    right_ref[0:2] = right_in[...]
    low_ref[0:2] = low_in[...]
    high_ref[0:2] = high_in[...]
    slot = iota((8, RUN), 1) // 4

    def layer(l, _):
        sides = [jnp.zeros((8, RUN), F32) for _ in range(2)]
        for g in range(GROUPS):
            for h in range(2):
                cols = slice(h * RUN, (h + 1) * RUN)
                start = pl.multiple_of(l * 512 + g * 16 + h * 8, 8)
                total = (acc0[pl.ds(start, 8), :] + acc1[pl.ds(start, 8), :]) + (
                    acc2[pl.ds(start, 8), :] + acc3[pl.ds(start, 8), :]
                )
                field_ref[l, 8 * g : 8 * g + 8, cols] = total
                if h == 0:
                    sides[0] = fold_left(sides[0], total, g, slot)
                else:
                    sides[1] = fold_right(sides[1], total, g, slot)
                if g == 0:
                    low_ref[2, l, :, cols] = total[:4]
                if g == GROUPS - 1:
                    high_ref[2, l, :, cols] = total[4:]
        left_ref[2, l] = sides[0]
        right_ref[2, l] = sides[1]
        return 0

    lax.fori_loop(0, LAYERS, layer, 0)


def gather(incoming, left, right, low, high):
    vmem = pl.BlockSpec(memory_space=pltpu.VMEM)
    return pl.pallas_call(
        gather_kernel,
        out_shape=(
            jax.ShapeDtypeStruct((LAYERS, NX, NY), F32),
            jax.ShapeDtypeStruct((3, LAYERS, 8, RUN), F32),
            jax.ShapeDtypeStruct((3, LAYERS, 8, RUN), F32),
            jax.ShapeDtypeStruct((3, LAYERS, 4, NY), F32),
            jax.ShapeDtypeStruct((3, LAYERS, 4, NY), F32),
        ),
        in_specs=[vmem] * 5,
        out_specs=(vmem,) * 5,
        scratch_shapes=[pltpu.VMEM((POSITIONS + 8, RUN), F32)] * ACCS
        + [
            pltpu.VMEM((128, RUN), jnp.int32),
            pltpu.SMEM((128, RUN), jnp.int32),
            pltpu.SemaphoreType.DMA,
        ],
        compiler_params=pltpu.CompilerParams(vmem_limit_bytes=VMEM_LIMIT),
    )(incoming, left, right, low, high)


def corner_kernel(from_left, from_right, low_in, high_in, low_ref, high_ref):
    slot = iota((8, RUN), 1) // 4
    for l in range(LAYERS):
        low = jnp.zeros((8, RUN), F32)
        high = jnp.zeros((8, RUN), F32)
        for q in range(3):
            for side, ref in enumerate((from_left, from_right)):
                k = 2 * q + side
                v = ref[q, l]
                low = jnp.where(slot == k, pltpu.roll(v, (4 * k) % RUN, 1), low)
                high = jnp.where(slot == k, pltpu.roll(v, (4 * k + 4) % RUN, 1), high)
            low_ref[l, :, q * NY : (q + 1) * NY] = low_in[q, l]
            high_ref[l, :, q * NY : (q + 1) * NY] = high_in[q, l]
        low_ref[l, :, 3 * NY :] = low[:4]
        high_ref[l, :, 3 * NY :] = high[4:]


def corners(from_left, from_right, low, high):
    vmem = pl.BlockSpec(memory_space=pltpu.VMEM)
    shape = jax.ShapeDtypeStruct((LAYERS, 4, 3 * NY + RUN), F32)
    return pl.pallas_call(
        corner_kernel,
        out_shape=(shape, shape),
        in_specs=[vmem] * 4,
        out_specs=(vmem,) * 2,
    )(from_left, from_right, low, high)


def sweep_kernel(
    kind_ref, slope_ref, flag_ref, warmth_hbm, q_hbm, field_hbm, from_left, from_right, from_low, from_high,
    out_hbm,
    warm_a, warm_b, q_ext, field_ext, r_row, f_row, g_row, sem,
):
    bodies = (warmth_hbm, q_hbm, field_hbm)
    exts = (warm_a, q_ext, field_ext)
    copies = []
    for k in range(3):
        for l in range(LAYERS):
            for h in range(2):
                copies.append(
                    pltpu.make_async_copy(
                        bodies[k].at[l, :, pl.ds(h * RUN, RUN)],
                        exts[k].at[l, h, pl.ds(BASE, NX), :],
                        sem.at[k, l, h],
                    )
                )
    for c in copies:
        c.start()
    has_left = flag_ref[0] > 0
    has_right = flag_ref[1] > 0
    has_low = flag_ref[2] > 0
    has_high = flag_ref[3] > 0
    fills = (0.0, WALL, 0.0)
    lane = iota((8, RUN), 1)
    first_half = lane < 64

    def halo(l, _):
        for k in range(3):
            v = jnp.where(has_left, from_left[k, l], fills[k])
            w = jnp.where(has_right, from_right[k, l], fills[k])
            v = pltpu.roll(v, RUN - 4, 1)
            for g in range(GROUPS):
                shift = (RUN - 4 * g) % RUN
                third = jnp.where(first_half, pltpu.roll(w, shift, 1), pltpu.roll(v, shift, 1))
                exts[k][l, 2, BASE + 8 * g : BASE + 8 * g + 8, :] = third
            for ref, present, row in (
                (from_low, has_low, BASE - 4),
                (from_high, has_high, BASE + NX),
            ):
                for h in range(2):
                    main = ref[l, :, k * NY + h * RUN : k * NY + (h + 1) * RUN]
                    exts[k][l, h, row : row + 4, :] = jnp.where(present, main, fills[k])
                c = ref[l, :, 3 * NY :]
                cl = pltpu.roll(c, (RUN - (8 * k + 4)) % RUN, 1)
                cr = pltpu.roll(c, (RUN - (8 * k + 4)) % RUN, 1)
                cl = jnp.where(present & has_left, cl, fills[k])
                cr = jnp.where(present & has_right, cr, fills[k])
                exts[k][l, 2, row : row + 4, :] = jnp.where(first_half[:4], cr, cl)
        return 0

    lax.fori_loop(0, LAYERS, halo, 0)
    for c in copies:
        c.wait()

    last = lane == RUN - 1
    first = lane == 0

    def up(v):
        s = [pltpu.roll(x, RUN - 1, 1) for x in v]
        return [jnp.where(last, s[(h + 1) % 3], s[h]) for h in range(3)]

    def down(v):
        s = [pltpu.roll(x, 1, 1) for x in v]
        return [jnp.where(first, s[(h + 2) % 3], s[h]) for h in range(3)]

    def rcp(x):
        return pl.reciprocal(x, approx=True)

    slopes = [slope_ref[kind_ref[l]] for l in range(LAYERS)]

    def one_sweep(src, dst, top, stride):
        def load(ref, l, j):
            return [ref[l, h, pl.ds(top + j, 8, stride=stride), :] for h in range(3)]

        def resist(q, t, c):
            return [a * (1.0 + c * b) for a, b in zip(q, t)]

        for l in range(LAYERS):
            t0 = load(src, l, -1)
            t1 = load(src, l, 0)
            r0 = resist(load(q_ext, l, -1), t0, slopes[l])
            r1 = resist(load(q_ext, l, 0), t1, slopes[l])
            for h in range(3):
                g = rcp(r0[h] + r1[h])
                r_row[l, h] = r1[h]
                g_row[l, h] = g
                f_row[l, h] = g * (t1[h] - t0[h])

        def step(j, _):
            fz = gz = None
            t = load(src, 0, j)
            r = [r_row[0, h] for h in range(3)]
            for l in range(LAYERS):
                tn = load(src, l, j + 1)
                rn = resist(load(q_ext, l, j + 1), tn, slopes[l])
                power = load(field_ext, l, j)
                if l < LAYERS - 1:
                    t_above = load(src, l + 1, j)
                    r_above = [r_row[l + 1, h] for h in range(3)]
                net = []
                den = []
                for h in range(3):
                    gx = rcp(r[h] + rn[h])
                    fx = gx * (tn[h] - t[h])
                    net.append(fx - f_row[l, h])
                    den.append(gx + g_row[l, h])
                    r_row[l, h] = rn[h]
                    f_row[l, h] = fx
                    g_row[l, h] = gx
                ru = up(r)
                tu = up(t)
                gy = [rcp(r[h] + ru[h]) for h in range(3)]
                fy = [gy[h] * (tu[h] - t[h]) for h in range(3)]
                gd = down(gy)
                fd = down(fy)
                for h in range(3):
                    net[h] = net[h] + (fy[h] - fd[h])
                    den[h] = den[h] + (gy[h] + gd[h])
                if l > 0:
                    for h in range(3):
                        net[h] = net[h] - fz[h]
                        den[h] = den[h] + gz[h]
                else:
                    for h in range(3):
                        net[h] = net[h] - 2.0 * t[h]
                        den[h] = den[h] + 2.0
                if l < LAYERS - 1:
                    gz = [0.5 * rcp(r[h] + r_above[h]) for h in range(3)]
                    fz = [gz[h] * (t_above[h] - t[h]) for h in range(3)]
                    for h in range(3):
                        net[h] = net[h] + fz[h]
                        den[h] = den[h] + gz[h]
                for h in range(3):
                    fresh = t[h] + (0.5 * power[h] + net[h]) * rcp(den[h])
                    dst[l, h, pl.ds(top + j, 8, stride=stride), :] = fresh
                if l < LAYERS - 1:
                    t = t_above
                    r = r_above
            return 0

        lax.fori_loop(0, stride, step, 0)

    one_sweep(warm_a, warm_b, BASE - 4, 33)
    one_sweep(warm_b, warm_a, BASE - 4, 33)
    one_sweep(warm_a, warm_b, BASE - 4, 33)
    copies = [
        pltpu.make_async_copy(
            warm_b.at[l, h, pl.ds(BASE, NX), :],
            out_hbm.at[l, :, pl.ds(h * RUN, RUN)],
            sem.at[0, l, h],
        )
        for l in range(LAYERS)
        for h in range(2)
    ]
    for c in copies:
        c.start()
    for c in copies:
        c.wait()


def sweeps(kind, slope, flags, warmth, q, field, from_left, from_right, from_low, from_high):
    vmem = pl.BlockSpec(memory_space=pltpu.VMEM)
    smem = pl.BlockSpec(memory_space=pltpu.SMEM)
    hbm = pl.BlockSpec(memory_space=pl.ANY)
    ext = pltpu.VMEM((LAYERS, 3, ROWS, RUN), F32)
    row = pltpu.VMEM((LAYERS, 3, 8, RUN), F32)
    return pl.pallas_call(
        sweep_kernel,
        out_shape=jax.ShapeDtypeStruct((LAYERS, NX, NY), F32),
        in_specs=[smem, smem, smem, hbm, hbm, hbm, vmem, vmem, vmem, vmem],
        out_specs=hbm,
        scratch_shapes=[ext, ext, ext, ext, row, row, row, pltpu.SemaphoreType.DMA((3, LAYERS, 2))],
        compiler_params=pltpu.CompilerParams(vmem_limit_bytes=VMEM_LIMIT),
    )(kind, slope, flags, warmth, q, field, from_left, from_right, from_low, from_high)


def ring(axis):
    n = lax.axis_size(axis)
    return [(i, (i + 1) % n) for i in range(n)], [((i + 1) % n, i) for i in range(n)]


def per_device(
    segment_wattage_table,
    segment_target_tile,
    occupied_slot_tally,
    segment_tile_position,
    stratum_substance,
    substance_transport_base,
    substance_thermal_slope,
    thermal_scaling_factor,
    starting_warmth_excess,
):
    tiles = 128
    outgoing = pack(
        occupied_slot_tally,
        segment_target_tile.reshape(-1, RUN),
        segment_tile_position.reshape(-1, RUN),
        segment_wattage_table,
    )
    incoming = lax.all_to_all(
        outgoing.reshape(tiles, 1, CHUNK * RUN), ("gx", "gy"), split_axis=0, concat_axis=0, tiled=True
    ).reshape(tiles * CHUNK, RUN)
    q, left, right, low, high = prepare(
        stratum_substance, substance_transport_base, starting_warmth_excess, thermal_scaling_factor
    )
    field, left, right, low, high = gather(incoming, left, right, low, high)
    ahead, behind = ring("gy")
    from_left = lax.ppermute(right, "gy", ahead)
    from_right = lax.ppermute(left, "gy", behind)
    low, high = corners(from_left, from_right, low, high)
    ahead, behind = ring("gx")
    from_low = lax.ppermute(high, "gx", ahead)
    from_high = lax.ppermute(low, "gx", behind)
    i = lax.axis_index("gx")
    k = lax.axis_index("gy")
    flags = jnp.stack(
        [k > 0, k < lax.axis_size("gy") - 1, i > 0, i < lax.axis_size("gx") - 1]
    ).astype(jnp.int32)
    final = sweeps(
        stratum_substance,
        substance_thermal_slope,
        flags,
        starting_warmth_excess,
        q,
        field,
        from_left,
        from_right,
        from_low,
        from_high,
    )
    return field, final


def solution(mesh):
    return jax.shard_map(
        per_device,
        mesh=mesh,
        in_specs=(
            P(("gx", "gy"), None),
            P(("gx", "gy")),
            P(("gx", "gy")),
            P(("gx", "gy")),
            P(),
            P(),
            P(),
            P(None, "gx", "gy"),
            P(None, "gx", "gy"),
        ),
        out_specs=(P(None, "gx", "gy"), P(None, "gx", "gy")),
        check_vma=False,
    )
```

profile of v0, /device:TPU:0, one launch (start us, length us, event | category | flops | bytes accessed | tf_op | source)
XLA Modules:
  0.0 142.3 jit_solution(17003902445965894595)
XLA Ops:
  1.3 23.4 %shard_map.104 = f32[6272,128]{1,0:T(8,128)} custom-call(s32[1]{0:T(128)S(6)} %copy.12.tally_ref, s32[32,128]{1,0:T(8,128)} %bitcast.10, s32[32,128]{1,0:T(8,128)} %bitcast.11, f32[4096,128]{1,0:T(8,128)} %table_ref.1), custom_call_target="tpu_custom_call" | custom-call | tf_op jit(solution)/shard_map/pallas_call | solution.py:83
  24.7 12.4 %all-to-all-start = ((f32[128,1,6272]{2,1,0:T(1,128)}), f32[128,1,6272]{2,1,0:T(1,128)S(1)}, u32[]{:S(2)}, u32[]{:S(2)}) async-start(f32[128,1,6272]{2,1,0:T(1,128)} %bitcast.9), calls=%async_computation | async-start | bytes 6422528 | tf_op jit(solution)/shard_map/all_to_all | solution.py:476
  37.1 5.3 %shard_map.105 = (f32[8,256,256]{2,1,0:T(8,128)}, f32[2,8,8,128]{3,2,1,0:T(8,128)}, f32[2,8,8,128]{3,2,1,0:T(8,128)}, f32[2,8,4,256]{3,2,1,0:T(4,128)}, f32[2,8,4,256]{3,2,1,0:T(4,128)}) custom-call(s32[8]{0:T(128)} %kind_ref.3, f32[4]{0:T(128)} %base_ref.1, f32[8,256,256]{2,1,0:T(8,128)} %warmth_hbm.1, f32[8,256,256]{2,1,0:T(8,128)} %scale_ref.1), custom_call_target="tpu_custom_call" | custom-call | flops 8000000 | bytes 6300000 | tf_op jit(solution)/shard_map/pallas_call | solution.py:148
  42.4 36.1 %all-to-all-done = f32[128,1,6272]{2,1,0:T(1,128)S(1)} async-done(((f32[128,1,6272]{2,1,0:T(1,128)}), f32[128,1,6272]{2,1,0:T(1,128)S(1)}, u32[]{:S(2)}, u32[]{:S(2)}) %all-to-all-start) | async-done | bytes 3211296 | tf_op jit(solution)/shard_map/all_to_all | solution.py:476
  78.5 0.0 copy-start
  78.5 1.7 %copy-done = f32[128,1,6272]{2,1,0:T(1,128)} copy-done((f32[128,1,6272]{2,1,0:T(1,128)}, f32[128,1,6272]{2,1,0:T(1,128)S(1)}, u32[]{:S(2)}) %copy-start) | copy-done | bytes 3211288
  80.2 15.1 %shard_map.106 = (f32[8,256,256]{2,1,0:T(8,128)}, f32[3,8,8,128]{3,2,1,0:T(8,128)}, f32[3,8,8,128]{3,2,1,0:T(8,128)}, f32[3,8,4,256]{3,2,1,0:T(4,128)}, f32[3,8,4,256]{3,2,1,0:T(4,128)}) custom-call(f32[6272,128]{1,0:T(8,128)} %bitcast.8, f32[2,8,8,128]{3,2,1,0:T(8,128)} %get-tuple-element.14.left_in, f32[2,8,8,128]{3,2,1,0:T(8,128)} %get-tuple-element.15.right_in, ...), custom_call_target="tpu_custom_call" | custom-call | tf_op jit(solution)/shard_map/pallas_call | solution.py:226
  95.2 2.2 %collective-permute-start = (f32[3,8,8,128]{3,2,1,0:T(8,128)}, f32[3,8,8,128]{3,2,1,0:T(8,128)S(1)}, u32[]{:S(2)}, u32[]{:S(2)}) collective-permute-start(f32[3,8,8,128]{3,2,1,0:T(8,128)} %get-tuple-element.20), channel_id=1, source_target_pairs={{0,1},{1,2},{2,3},{3,4},{4,5},{5,6},{6,7},{7,0},{8,9},{9,10},{10,1... | collective-permute-start | bytes 294920 | tf_op jit(solution)/shard_map/ppermute | solution.py:484
  97.4 3.5 %collective-permute-start.1 = (f32[3,8,8,128]{3,2,1,0:T(8,128)}, f32[3,8,8,128]{3,2,1,0:T(8,128)S(1)}, u32[]{:S(2)}, u32[]{:S(2)}) collective-permute-start(f32[3,8,8,128]{3,2,1,0:T(8,128)} %get-tuple-element.21), channel_id=1, source_target_pairs={{1,0},{2,1},{3,2},{4,3},{5,4},{6,5},{7,6},{0,7},{9,8},{10,9},{11,1... | collective-permute-start | bytes 294920 | tf_op jit(solution)/shard_map/ppermute | solution.py:485
  100.9 2.9 %collective-permute-done.from_left = f32[3,8,8,128]{3,2,1,0:T(8,128)S(1)} collective-permute-done((f32[3,8,8,128]{3,2,1,0:T(8,128)}, f32[3,8,8,128]{3,2,1,0:T(8,128)S(1)}, u32[]{:S(2)}, u32[]{:S(2)}) %collective-permute-start) | collective-permute-done | bytes 98336 | tf_op jit(solution)/shard_map/ppermute | solution.py:484
  103.8 0.0 copy-start.1
  103.8 0.2 collective-permute-done.1.from_right
  104.0 0.0 copy-start.2
  104.0 0.4 copy-done.1
  104.4 0.2 copy-done.2
  104.7 1.9 %shard_map.107 = (f32[8,4,896]{2,1,0:T(4,128)}, f32[8,4,896]{2,1,0:T(4,128)}) custom-call(f32[3,8,8,128]{3,2,1,0:T(8,128)} %copy-done.1, f32[3,8,8,128]{3,2,1,0:T(8,128)} %copy-done.2, f32[3,8,4,256]{3,2,1,0:T(4,128)} %get-tuple-element.22.low_in, f32[3,8,4,256]{3,2,1,0:T(4,128)} %get-tuple-element.23.high_in), custom_call_target="tpu_custom_call" | custom-call | tf_op jit(solution)/shard_map/pallas_call | solution.py:267
  106.5 0.0 collective-permute-start.2
  106.6 3.9 %collective-permute-start.3 = (f32[8,4,896]{2,1,0:T(4,128)}, f32[8,4,896]{2,1,0:T(4,128)S(1)}, u32[]{:S(2)}, u32[]{:S(2)}) collective-permute-start(f32[8,4,896]{2,1,0:T(4,128)} %get-tuple-element.25), channel_id=1, source_target_pairs={{8,0},{16,8},{24,16},{32,24},{40,32},{48,40},{56,48},{64,56},{72,6... | collective-permute-start | bytes 344072 | tf_op jit(solution)/shard_map/ppermute | solution.py:489
  110.4 0.6 add_convert_fusion.flag_ref
  111.0 2.1 %collective-permute-done.2.from_low = f32[8,4,896]{2,1,0:T(4,128)S(1)} collective-permute-done((f32[8,4,896]{2,1,0:T(4,128)}, f32[8,4,896]{2,1,0:T(4,128)S(1)}, u32[]{:S(2)}, u32[]{:S(2)}) %collective-permute-start.2) | collective-permute-done | bytes 114720 | tf_op jit(solution)/shard_map/ppermute | solution.py:488
  113.1 0.0 copy-start.3
  113.1 0.0 collective-permute-done.3.from_high
  113.1 0.0 copy-start.4
  113.1 0.6 copy-done.3
  113.7 0.1 copy-done.4
  113.8 28.6 %shard_map.108 = f32[8,256,256]{2,1,0:T(8,128)} custom-call(s32[8]{0:T(128)} %kind_ref.3, f32[4]{0:T(128)} %slope_ref.1, s32[4]{0:T(128)} %add_convert_fusion.flag_ref, f32[8,256,256]{2,1,0:T(8,128)} %warmth_hbm.1, f32[8,256,256]{2,1,0:T(8,128)} %get-tuple-element.19.q_hbm, f32[8,256,256]{2,1,0:T(8,128)} %get-tuple-element.12.field_hbm, ...), custom_call_target="tpu_custom_call" | custom-call | tf_op jit(solution)/shard_map/pallas_call | solution.py:443
Async XLA Ops:
  24.7 53.8 %all-to-all-start = ((f32[128,1,6272]{2,1,0:T(1,128)}), f32[128,1,6272]{2,1,0:T(1,128)S(1)}, u32[]{:S(2)}, u32[]{:S(2)}) async-start(f32[128,1,6272]{2,1,0:T(1,128)} %bitcast.9), calls=%async_computation | async-start | bytes 6422528 | tf_op jit(solution)/shard_map/all_to_all | solution.py:476
  78.5 1.7 %copy-start = (f32[128,1,6272]{2,1,0:T(1,128)}, f32[128,1,6272]{2,1,0:T(1,128)S(1)}, u32[]{:S(2)}) copy-start(f32[128,1,6272]{2,1,0:T(1,128)S(1)} %all-to-all-done) | copy-start | bytes 9633796
  95.2 8.6 %collective-permute-start = (f32[3,8,8,128]{3,2,1,0:T(8,128)}, f32[3,8,8,128]{3,2,1,0:T(8,128)S(1)}, u32[]{:S(2)}, u32[]{:S(2)}) collective-permute-start(f32[3,8,8,128]{3,2,1,0:T(8,128)} %get-tuple-element.20), channel_id=1, source_target_pairs={{0,1},{1,2},{2,3},{3,4},{4,5},{5,6},{6,7},{7,0},{8,9},{9,10},{10,1... | collective-permute-start | bytes 294920 | tf_op jit(solution)/shard_map/ppermute | solution.py:484
  97.4 6.6 %collective-permute-start.1 = (f32[3,8,8,128]{3,2,1,0:T(8,128)}, f32[3,8,8,128]{3,2,1,0:T(8,128)S(1)}, u32[]{:S(2)}, u32[]{:S(2)}) collective-permute-start(f32[3,8,8,128]{3,2,1,0:T(8,128)} %get-tuple-element.21), channel_id=1, source_target_pairs={{1,0},{2,1},{3,2},{4,3},{5,4},{6,5},{7,6},{0,7},{9,8},{10,9},{11,1... | collective-permute-start | bytes 294920 | tf_op jit(solution)/shard_map/ppermute | solution.py:485
  103.8 0.6 copy-start.1
  104.0 0.6 copy-start.2
  106.5 6.5 %collective-permute-start.2 = (f32[8,4,896]{2,1,0:T(4,128)}, f32[8,4,896]{2,1,0:T(4,128)S(1)}, u32[]{:S(2)}, u32[]{:S(2)}) collective-permute-start(f32[8,4,896]{2,1,0:T(4,128)} %get-tuple-element.24), channel_id=1, source_target_pairs={{0,8},{8,16},{16,24},{24,32},{32,40},{40,48},{48,56},{56,64},{64,7... | collective-permute-start | bytes 344072 | tf_op jit(solution)/shard_map/ppermute | solution.py:488
  106.6 6.5 %collective-permute-start.3 = (f32[8,4,896]{2,1,0:T(4,128)}, f32[8,4,896]{2,1,0:T(4,128)S(1)}, u32[]{:S(2)}, u32[]{:S(2)}) collective-permute-start(f32[8,4,896]{2,1,0:T(4,128)} %get-tuple-element.25), channel_id=1, source_target_pairs={{8,0},{16,8},{24,16},{32,24},{40,32},{48,40},{56,48},{64,56},{72,6... | collective-permute-start | bytes 344072 | tf_op jit(solution)/shard_map/ppermute | solution.py:489
  113.1 0.6 copy-start.3
  113.1 0.7 copy-start.4
where the time goes:
time: 143 us; the launch traced here: 142 us
  Pallas kernels  74.2 us (52%)
  waiting for transfers between devices  41.3 us (29%)
  starting transfers between devices  22 us (15%)
  local copies, waits for them, and re-layouts  3 us (2%)
    all_to_all x1, waiting for transfers between devices, per_device(): lax.all_to_all(outgoing.reshape(tiles, 1, CHUNK * RUN), ('gx', 'gy'), spl...  36.1 us
    pallas_call x1, Pallas kernels, sweeps(): pl.pallas_call(sweep_kernel, out_shape=jax.ShapeDtypeStruct((LAYERS, NX,...  28.6 us
    pallas_call x1, Pallas kernels, pack(): pl.pallas_call(pack_kernel, out_shape=jax.ShapeDtypeStruct((tiles * CHUNK...  23.4 us
    pallas_call x1, Pallas kernels, gather(): pl.pallas_call(gather_kernel, out_shape=(jax.ShapeDtypeStruct((LAYERS, NX...  15.1 us
    all_to_all x1, starting transfers between devices, per_device(): lax.all_to_all(outgoing.reshape(tiles, 1, CHUNK * RUN), ('gx', 'gy'), spl...  12.4 us
    pallas_call x1, Pallas kernels, prepare(): pl.pallas_call(prepare_kernel, out_shape=(jax.ShapeDtypeStruct(warmth.sha...  5.26 us
    ppermute x1, starting transfers between devices, per_device(): from_high = lax.ppermute(low, 'gx', behind)  3.85 us
    ppermute x1, starting transfers between devices, per_device(): from_right = lax.ppermute(left, 'gy', behind)  3.51 us
  transfers between devices with their start and end apart: 5, of which 4 were waited for; matrix products, arithmetic and copies ran while one was open for 0% of the time, Pallas kernels for 4%

commit v1 on v0

--- a/solution.py
+++ b/solution.py
@@ -14,7 +14,7 @@
 NY = 256
 GROUPS = NX // 8
 POSITIONS = LAYERS * NX * NY // RUN
-ACCS = 4
+ACCS = 8
 WALL = 1e30
 BASE = 16
 ROWS = 280
@@ -27,7 +27,11 @@
     return lax.broadcasted_iota(jnp.int32, shape, dim)
 
 
-def pack_kernel(tally_ref, target_ref, place_ref, table_ref, out_ref, dest_v, dest_s, sem):
+def pack_kernel(
+    tally_ref, target_ref, place_ref, table_hbm, out_ref, table_ref, dest_v, dest_s, sem, table_sem
+):
+    load = pltpu.make_async_copy(table_hbm, table_ref, table_sem)
+    load.start()
     tally = tally_ref[0]
     tiles = 128
     sub = iota((tiles, RUN), 0)
@@ -60,20 +64,20 @@
         return seen + run[:, RUN:], placed
 
     zero = jnp.zeros((tiles, RUN), F32)
-    seen, placed = lax.fori_loop(0, target_ref.shape[0], rank_group, (zero, zero))
+    seen, placed = lax.fori_loop(0, 32, rank_group, (zero, zero), unroll=32)
     placed = placed + 64.0 * pltpu.roll(placed, 64, 1)
     copy = pltpu.make_async_copy(dest_v, dest_s, sem)
     copy.start()
     copy.wait()
 
-    def move(j, _):
-        for k in range(16):
-            row = j * 16 + k
-            d = dest_s[j // 8, (j % 8) * 16 + k]
-            out_ref[pl.ds(d, 1), :] = table_ref[pl.ds(row, 1), :]
+    load.wait()
+
+    def move(g, _):
+        for k in range(RUN):
+            out_ref[pl.ds(dest_s[g, k], 1), :] = table_ref[pl.ds(g * RUN + k, 1), :]
         return 0
 
-    lax.fori_loop(0, (tally + 15) // 16, move, 0)
+    lax.fori_loop(0, (tally + RUN - 1) // RUN, move, 0)
     for t in range(tiles):
         out_ref[t * CHUNK + CAP : t * CHUNK + CAP + 1, :] = placed[t : t + 1, :]
 
@@ -87,12 +91,14 @@
             pl.BlockSpec(memory_space=pltpu.SMEM),
             pl.BlockSpec(memory_space=pltpu.VMEM),
             pl.BlockSpec(memory_space=pltpu.VMEM),
-            pl.BlockSpec(memory_space=pltpu.VMEM),
+            pl.BlockSpec(memory_space=pl.ANY),
         ],
         out_specs=pl.BlockSpec(memory_space=pltpu.VMEM),
         scratch_shapes=[
+            pltpu.VMEM((32 * RUN, RUN), F32),
             pltpu.VMEM((32, RUN), jnp.int32),
             pltpu.SMEM((32, RUN), jnp.int32),
+            pltpu.SemaphoreType.DMA,
             pltpu.SemaphoreType.DMA,
         ],
         compiler_params=pltpu.CompilerParams(vmem_limit_bytes=VMEM_LIMIT),
@@ -162,17 +168,21 @@
 
 
 def gather_kernel(
-    inc_ref, left_in, right_in, low_in, high_in,
-    field_ref, left_ref, right_ref, low_ref, high_ref,
-    acc0, acc1, acc2, acc3, spot_v, spot_s, sem,
+    flag_ref, inc_hbm, left_in, right_in, low_in, high_in,
+    field_hbm, first_ref, second_ref, low_ref, high_ref,
+    inc_ref, field_ref, spot_v, spot_s, inc_sem, spot_sem, field_sem, *accs,
 ):
-    accs = (acc0, acc1, acc2, acc3)
     tiles = 128
-    for t in range(tiles):
-        row = inc_ref[t * CHUNK + CAP : t * CHUNK + CAP + 1, :]
-        spot_v[t : t + 1, :] = jnp.where(row > 0.5, row.astype(jnp.int32) - 1, POSITIONS)
-    copy = pltpu.make_async_copy(spot_v, spot_s, sem)
-    copy.start()
+    parts = 8
+    size = tiles * CHUNK // parts
+    loads = [
+        pltpu.make_async_copy(
+            inc_hbm.at[pl.ds(i * size, size), :], inc_ref.at[pl.ds(i * size, size), :], inc_sem.at[i]
+        )
+        for i in range(parts)
+    ]
+    for c in loads:
+        c.start()
 
     def clear(i, _):
         for acc in accs:
@@ -180,21 +190,37 @@
         return 0
 
     lax.fori_loop(0, POSITIONS // 64, clear, 0)
+    for c in loads:
+        c.wait()
+    for t in range(tiles):
+        row = inc_ref[t * CHUNK + CAP : t * CHUNK + CAP + 1, :]
+        spot_v[t : t + 1, :] = jnp.where(row > 0.5, row.astype(jnp.int32) - 1, POSITIONS)
+    copy = pltpu.make_async_copy(spot_v, spot_s, spot_sem)
+    copy.start()
     copy.wait()
 
     def source(s, _):
         for p in range(CAP):
-            o = spot_s[s, p]
             acc = accs[p % ACCS]
-            acc[pl.ds(o, 1), :] += inc_ref[pl.ds(s * CHUNK + p, 1), :]
+            acc[pl.ds(spot_s[s, p], 1), :] += inc_ref[pl.ds(s * CHUNK + p, 1), :]
         return 0
 
     lax.fori_loop(0, tiles, source, 0)
-    left_ref[0:2] = left_in[...]
-    right_ref[0:2] = right_in[...]
+    even = flag_ref[4] > 0
+
+    def send(k, l, left, right):
+        first_ref[k, l] = jnp.where(even, right, left)
+        second_ref[k, l] = jnp.where(even, left, right)
+
+    for k in range(2):
+        for l in range(LAYERS):
+            send(k, l, left_in[k, l], right_in[k, l])
     low_ref[0:2] = low_in[...]
     high_ref[0:2] = high_in[...]
     slot = iota((8, RUN), 1) // 4
+
+    def stored(l):
+        return pltpu.make_async_copy(field_ref.at[l], field_hbm.at[l], field_sem.at[l])
 
     def layer(l, _):
         sides = [jnp.zeros((8, RUN), F32) for _ in range(2)]
@@ -202,9 +228,10 @@
             for h in range(2):
                 cols = slice(h * RUN, (h + 1) * RUN)
                 start = pl.multiple_of(l * 512 + g * 16 + h * 8, 8)
-                total = (acc0[pl.ds(start, 8), :] + acc1[pl.ds(start, 8), :]) + (
-                    acc2[pl.ds(start, 8), :] + acc3[pl.ds(start, 8), :]
-                )
+                terms = [acc[pl.ds(start, 8), :] for acc in accs]
+                while len(terms) > 1:
+                    terms = [sum(terms[i : i + 2]) for i in range(0, len(terms), 2)]
+                total = terms[0]
                 field_ref[l, 8 * g : 8 * g + 8, cols] = total
                 if h == 0:
                     sides[0] = fold_left(sides[0], total, g, slot)
@@ -214,15 +241,19 @@
                     low_ref[2, l, :, cols] = total[:4]
                 if g == GROUPS - 1:
                     high_ref[2, l, :, cols] = total[4:]
-        left_ref[2, l] = sides[0]
-        right_ref[2, l] = sides[1]
+        send(2, l, sides[0], sides[1])
+        stored(l).start()
         return 0
 
     lax.fori_loop(0, LAYERS, layer, 0)
-
-
-def gather(incoming, left, right, low, high):
+    for l in range(LAYERS):
+        stored(l).wait()
+
+
+def gather(flags, incoming, left, right, low, high):
     vmem = pl.BlockSpec(memory_space=pltpu.VMEM)
+    hbm = pl.BlockSpec(memory_space=pl.ANY)
+    smem = pl.BlockSpec(memory_space=pltpu.SMEM)
     return pl.pallas_call(
         gather_kernel,
         out_shape=(
@@ -232,50 +263,62 @@
             jax.ShapeDtypeStruct((3, LAYERS, 4, NY), F32),
             jax.ShapeDtypeStruct((3, LAYERS, 4, NY), F32),
         ),
-        in_specs=[vmem] * 5,
-        out_specs=(vmem,) * 5,
-        scratch_shapes=[pltpu.VMEM((POSITIONS + 8, RUN), F32)] * ACCS
-        + [
+        in_specs=[smem, hbm] + [vmem] * 4,
+        out_specs=(hbm,) + (vmem,) * 4,
+        scratch_shapes=[
+            pltpu.VMEM((128 * CHUNK, RUN), F32),
+            pltpu.VMEM((LAYERS, NX, NY), F32),
             pltpu.VMEM((128, RUN), jnp.int32),
             pltpu.SMEM((128, RUN), jnp.int32),
+            pltpu.SemaphoreType.DMA((8,)),
             pltpu.SemaphoreType.DMA,
-        ],
+            pltpu.SemaphoreType.DMA((LAYERS,)),
+        ]
+        + [pltpu.VMEM((POSITIONS + 8, RUN), F32)] * ACCS,
         compiler_params=pltpu.CompilerParams(vmem_limit_bytes=VMEM_LIMIT),
-    )(incoming, left, right, low, high)
-
-
-def corner_kernel(from_left, from_right, low_in, high_in, low_ref, high_ref):
+    )(flags, incoming, left, right, low, high)
+
+
+def corner_kernel(flag_ref, first_in, second_in, low_in, high_in, first_ref, second_ref):
     slot = iota((8, RUN), 1) // 4
+    even_y = flag_ref[4] > 0
+    even_x = flag_ref[5] > 0
+
+    def send(l, cols, low, high):
+        first_ref[l, :, cols] = jnp.where(even_x, high, low)
+        second_ref[l, :, cols] = jnp.where(even_x, low, high)
+
     for l in range(LAYERS):
         low = jnp.zeros((8, RUN), F32)
         high = jnp.zeros((8, RUN), F32)
         for q in range(3):
-            for side, ref in enumerate((from_left, from_right)):
+            a = first_in[q, l]
+            b = second_in[q, l]
+            for side in range(2):
                 k = 2 * q + side
-                v = ref[q, l]
+                v = jnp.where(even_y, a, b) if side else jnp.where(even_y, b, a)
                 low = jnp.where(slot == k, pltpu.roll(v, (4 * k) % RUN, 1), low)
                 high = jnp.where(slot == k, pltpu.roll(v, (4 * k + 4) % RUN, 1), high)
-            low_ref[l, :, q * NY : (q + 1) * NY] = low_in[q, l]
-            high_ref[l, :, q * NY : (q + 1) * NY] = high_in[q, l]
-        low_ref[l, :, 3 * NY :] = low[:4]
-        high_ref[l, :, 3 * NY :] = high[4:]
-
-
-def corners(from_left, from_right, low, high):
+            send(l, slice(q * NY, (q + 1) * NY), low_in[q, l], high_in[q, l])
+        send(l, slice(3 * NY, 3 * NY + RUN), low[:4], high[4:])
+
+
+def corners(flags, first, second, low, high):
+    smem = pl.BlockSpec(memory_space=pltpu.SMEM)
     vmem = pl.BlockSpec(memory_space=pltpu.VMEM)
     shape = jax.ShapeDtypeStruct((LAYERS, 4, 3 * NY + RUN), F32)
     return pl.pallas_call(
         corner_kernel,
         out_shape=(shape, shape),
-        in_specs=[vmem] * 4,
+        in_specs=[smem] + [vmem] * 4,
         out_specs=(vmem,) * 2,
-    )(from_left, from_right, low, high)
+    )(flags, first, second, low, high)
 
 
 def sweep_kernel(
-    kind_ref, slope_ref, flag_ref, warmth_hbm, q_hbm, field_hbm, from_left, from_right, from_low, from_high,
+    kind_ref, slope_ref, flag_ref, warmth_hbm, q_hbm, field_hbm, first_y, second_y, first_x, second_x,
     out_hbm,
-    warm_a, warm_b, q_ext, field_ext, r_row, f_row, g_row, sem,
+    warm_a, warm_b, q_ext, field_ext, r_row, f_row, g_row, shifted, sem,
 ):
     bodies = (warmth_hbm, q_hbm, field_hbm)
     exts = (warm_a, q_ext, field_ext)
@@ -296,31 +339,36 @@
     has_right = flag_ref[1] > 0
     has_low = flag_ref[2] > 0
     has_high = flag_ref[3] > 0
+    even_y = flag_ref[4] > 0
+    even_x = flag_ref[5] > 0
     fills = (0.0, WALL, 0.0)
     lane = iota((8, RUN), 1)
     first_half = lane < 64
 
     def halo(l, _):
         for k in range(3):
-            v = jnp.where(has_left, from_left[k, l], fills[k])
-            w = jnp.where(has_right, from_right[k, l], fills[k])
+            a = first_y[k, l]
+            b = second_y[k, l]
+            v = jnp.where(has_left, jnp.where(even_y, b, a), fills[k])
+            w = jnp.where(has_right, jnp.where(even_y, a, b), fills[k])
             v = pltpu.roll(v, RUN - 4, 1)
             for g in range(GROUPS):
                 shift = (RUN - 4 * g) % RUN
                 third = jnp.where(first_half, pltpu.roll(w, shift, 1), pltpu.roll(v, shift, 1))
                 exts[k][l, 2, BASE + 8 * g : BASE + 8 * g + 8, :] = third
-            for ref, present, row in (
-                (from_low, has_low, BASE - 4),
-                (from_high, has_high, BASE + NX),
-            ):
+            for high, present, row in ((False, has_low, BASE - 4), (True, has_high, BASE + NX)):
+
+                def received(cols):
+                    a = first_x[l, :, cols]
+                    b = second_x[l, :, cols]
+                    return jnp.where(even_x, a, b) if high else jnp.where(even_x, b, a)
+
                 for h in range(2):
-                    main = ref[l, :, k * NY + h * RUN : k * NY + (h + 1) * RUN]
+                    main = received(slice(k * NY + h * RUN, k * NY + (h + 1) * RUN))
                     exts[k][l, h, row : row + 4, :] = jnp.where(present, main, fills[k])
-                c = ref[l, :, 3 * NY :]
-                cl = pltpu.roll(c, (RUN - (8 * k + 4)) % RUN, 1)
-                cr = pltpu.roll(c, (RUN - (8 * k + 4)) % RUN, 1)
-                cl = jnp.where(present & has_left, cl, fills[k])
-                cr = jnp.where(present & has_right, cr, fills[k])
+                c = pltpu.roll(received(slice(3 * NY, 3 * NY + RUN)), RUN - (8 * k + 4), 1)
+                cl = jnp.where(present & has_left, c, fills[k])
+                cr = jnp.where(present & has_right, c, fills[k])
                 exts[k][l, 2, row : row + 4, :] = jnp.where(first_half[:4], cr, cl)
         return 0
 
@@ -350,6 +398,11 @@
 
         def resist(q, t, c):
             return [a * (1.0 + c * b) for a, b in zip(q, t)]
+
+        def shift(l, r, t):
+            for i, v in enumerate((up(r), down(r), up(t), down(t))):
+                for h in range(3):
+                    shifted[i, l, h] = v[h]
 
         for l in range(LAYERS):
             t0 = load(src, l, -1)
@@ -361,6 +414,7 @@
                 r_row[l, h] = r1[h]
                 g_row[l, h] = g
                 f_row[l, h] = g * (t1[h] - t0[h])
+            shift(l, r1, t1)
 
         def step(j, _):
             fz = gz = None
@@ -383,15 +437,13 @@
                     r_row[l, h] = rn[h]
                     f_row[l, h] = fx
                     g_row[l, h] = gx
-                ru = up(r)
-                tu = up(t)
-                gy = [rcp(r[h] + ru[h]) for h in range(3)]
-                fy = [gy[h] * (tu[h] - t[h]) for h in range(3)]
-                gd = down(gy)
-                fd = down(fy)
                 for h in range(3):
-                    net[h] = net[h] + (fy[h] - fd[h])
-                    den[h] = den[h] + (gy[h] + gd[h])
+                    ru, rd, tu, td = (shifted[i, l, h] for i in range(4))
+                    gu = rcp(r[h] + ru)
+                    gd = rcp(r[h] + rd)
+                    net[h] = net[h] + (gu * (tu - t[h]) + gd * (td - t[h]))
+                    den[h] = den[h] + (gu + gd)
+                shift(l, rn, tn)
                 if l > 0:
                     for h in range(3):
                         net[h] = net[h] - fz[h]
@@ -434,7 +486,7 @@
         c.wait()
 
 
-def sweeps(kind, slope, flags, warmth, q, field, from_left, from_right, from_low, from_high):
+def sweeps(kind, slope, flags, warmth, q, field, first_y, second_y, first_x, second_x):
     vmem = pl.BlockSpec(memory_space=pltpu.VMEM)
     smem = pl.BlockSpec(memory_space=pltpu.SMEM)
     hbm = pl.BlockSpec(memory_space=pl.ANY)
@@ -445,14 +497,26 @@
         out_shape=jax.ShapeDtypeStruct((LAYERS, NX, NY), F32),
         in_specs=[smem, smem, smem, hbm, hbm, hbm, vmem, vmem, vmem, vmem],
         out_specs=hbm,
-        scratch_shapes=[ext, ext, ext, ext, row, row, row, pltpu.SemaphoreType.DMA((3, LAYERS, 2))],
+        scratch_shapes=[
+            ext,
+            ext,
+            ext,
+            ext,
+            row,
+            row,
+            row,
+            pltpu.VMEM((4, LAYERS, 3, 8, RUN), F32),
+            pltpu.SemaphoreType.DMA((3, LAYERS, 2)),
+        ],
         compiler_params=pltpu.CompilerParams(vmem_limit_bytes=VMEM_LIMIT),
-    )(kind, slope, flags, warmth, q, field, from_left, from_right, from_low, from_high)
-
-
-def ring(axis):
+    )(kind, slope, flags, warmth, q, field, first_y, second_y, first_x, second_x)
+
+
+def swap(axis, first, second):
     n = lax.axis_size(axis)
-    return [(i, (i + 1) % n) for i in range(n)], [((i + 1) % n, i) for i in range(n)]
+    pairs = [(i, i ^ 1) for i in range(n)]
+    others = [(i, (((i + 1) ^ 1) - 1) % n) for i in range(n)]
+    return lax.ppermute(first, axis, pairs), lax.ppermute(second, axis, others)
 
 
 def per_device(
@@ -479,19 +543,22 @@
     q, left, right, low, high = prepare(
         stratum_substance, substance_transport_base, starting_warmth_excess, thermal_scaling_factor
     )
-    field, left, right, low, high = gather(incoming, left, right, low, high)
-    ahead, behind = ring("gy")
-    from_left = lax.ppermute(right, "gy", ahead)
-    from_right = lax.ppermute(left, "gy", behind)
-    low, high = corners(from_left, from_right, low, high)
-    ahead, behind = ring("gx")
-    from_low = lax.ppermute(high, "gx", ahead)
-    from_high = lax.ppermute(low, "gx", behind)
     i = lax.axis_index("gx")
     k = lax.axis_index("gy")
     flags = jnp.stack(
-        [k > 0, k < lax.axis_size("gy") - 1, i > 0, i < lax.axis_size("gx") - 1]
+        [
+            k > 0,
+            k < lax.axis_size("gy") - 1,
+            i > 0,
+            i < lax.axis_size("gx") - 1,
+            k % 2 == 0,
+            i % 2 == 0,
+        ]
     ).astype(jnp.int32)
+    field, first, second, low, high = gather(flags, incoming, left, right, low, high)
+    first_y, second_y = swap("gy", first, second)
+    first, second = corners(flags, first_y, second_y, low, high)
+    first_x, second_x = swap("gx", first, second)
     final = sweeps(
         stratum_substance,
         substance_thermal_slope,
@@ -499,10 +566,10 @@
         starting_warmth_excess,
         q,
         field,
-        from_left,
-        from_right,
-        from_low,
-        from_high,
+        first_y,
+        second_y,
+        first_x,
+        second_x,
     )
     return field, final
 

time: 143 us -> 122 us (0.85)
  Pallas kernels: 74.2 us -> 52.9 us
  waiting for transfers between devices: 41.3 us -> 47.7 us
  starting transfers between devices: 22 us -> 16.1 us
    pallas_call x1, Pallas kernels: 23.4 us -> 7.74 us  [pack(): pl.pallas_call(pack_kernel, out_shape=jax.ShapeDtypeStruct((tiles * CHUNK...]
    ppermute x4, waiting for transfers between devices: 5.18 us -> 12.2 us  [the longest x2 9.13 us: swap(): lax.ppermute(second, axis, others)]
    ppermute x4, starting transfers between devices: 9.56 us -> 4.99 us  [the longest x2 2.78 us: swap(): lax.ppermute(second, axis, others)]
    pallas_call x1, Pallas kernels: 28.6 us -> 24.6 us  [sweeps(): pl.pallas_call(sweep_kernel, out_shape=jax.ShapeDtypeStruct((LAYERS, NX,...]
    pallas_call x1, Pallas kernels: 15.1 us -> 13.4 us  [gather(): pl.pallas_call(gather_kernel, out_shape=(jax.ShapeDtypeStruct((LAYERS, NX...]
  transfers between devices with their start and end apart: 5 -> 5, of which waited for: 4 -> 5; matrix products, arithmetic and copies ran while one was open for 0% -> 1% of each run, Pallas kernels for 4% -> 4%
where the time goes in v1:
time: 122 us
  Pallas kernels  52.9 us (43%)
  waiting for transfers between devices  47.7 us (39%)
  starting transfers between devices  16.1 us (13%)
  local copies, waits for them, and re-layouts  3.05 us (2%)
  between operations  1.34 us (1%)
    all_to_all x1, waiting for transfers between devices, per_device(): lax.all_to_all(outgoing.reshape(tiles, 1, CHUNK * RUN), ('gx', 'gy'), spl...  35.5 us
    pallas_call x1, Pallas kernels, sweeps(): pl.pallas_call(sweep_kernel, out_shape=jax.ShapeDtypeStruct((LAYERS, NX,...  24.6 us
    pallas_call x1, Pallas kernels, gather(): pl.pallas_call(gather_kernel, out_shape=(jax.ShapeDtypeStruct((LAYERS, NX...  13.4 us
    all_to_all x1, starting transfers between devices, per_device(): lax.all_to_all(outgoing.reshape(tiles, 1, CHUNK * RUN), ('gx', 'gy'), spl...  11.1 us
    ppermute x2, waiting for transfers between devices, swap(): lax.ppermute(second, axis, others)  9.13 us
    pallas_call x1, Pallas kernels, pack(): pl.pallas_call(pack_kernel, out_shape=jax.ShapeDtypeStruct((tiles * CHUNK...  7.74 us
    pallas_call x1, Pallas kernels, prepare(): pl.pallas_call(prepare_kernel, out_shape=(jax.ShapeDtypeStruct(warmth.sha...  5.25 us
    ppermute x2, waiting for transfers between devices, swap(): lax.ppermute(first, axis, pairs)  3.06 us
  transfers between devices with their start and end apart: 5, of which 5 were waited for; matrix products, arithmetic and copies ran while one was open for 1% of the time, Pallas kernels for 4%

profile of v1, /device:TPU:0, one launch (start us, length us, event | category | flops | bytes accessed | tf_op | source)
XLA Modules:
  0.0 121.6 jit_solution(2334580675721441790)
XLA Ops:
  1.3 7.7 %shard_map.104 = f32[6272,128]{1,0:T(8,128)} custom-call(s32[1]{0:T(128)S(6)} %copy.12.tally_ref, s32[32,128]{1,0:T(8,128)} %bitcast.12, s32[32,128]{1,0:T(8,128)} %bitcast.13, f32[4096,128]{1,0:T(8,128)} %table_hbm.1), custom_call_target="tpu_custom_call" | custom-call | tf_op jit(solution)/shard_map/pallas_call | solution.py:87
  9.0 11.1 %all-to-all-start = ((f32[128,1,6272]{2,1,0:T(1,128)}), f32[128,1,6272]{2,1,0:T(1,128)S(1)}, u32[]{:S(2)}, u32[]{:S(2)}) async-start(f32[128,1,6272]{2,1,0:T(1,128)} %bitcast.11), calls=%async_computation | async-start | bytes 6422528 | tf_op jit(solution)/shard_map/all_to_all | solution.py:540
  20.2 0.1 stack.27
  20.3 0.5 convert_element_type.3.flag_ref
  20.8 5.3 %shard_map.105 = (f32[8,256,256]{2,1,0:T(8,128)}, f32[2,8,8,128]{3,2,1,0:T(8,128)}, f32[2,8,8,128]{3,2,1,0:T(8,128)}, f32[2,8,4,256]{3,2,1,0:T(4,128)}, f32[2,8,4,256]{3,2,1,0:T(4,128)}) custom-call(s32[8]{0:T(128)} %kind_ref.3, f32[4]{0:T(128)} %base_ref.1, f32[8,256,256]{2,1,0:T(8,128)} %warmth_hbm.1, f32[8,256,256]{2,1,0:T(8,128)} %scale_ref.1), custom_call_target="tpu_custom_call" | custom-call | flops 8000000 | bytes 6300000 | tf_op jit(solution)/shard_map/pallas_call | solution.py:154
  26.1 35.5 %all-to-all-done = f32[128,1,6272]{2,1,0:T(1,128)S(1)} async-done(((f32[128,1,6272]{2,1,0:T(1,128)}), f32[128,1,6272]{2,1,0:T(1,128)S(1)}, u32[]{:S(2)}, u32[]{:S(2)}) %all-to-all-start) | async-done | bytes 3211296 | tf_op jit(solution)/shard_map/all_to_all | solution.py:540
  61.6 0.0 copy-start
  61.6 1.7 %copy-done = f32[128,1,6272]{2,1,0:T(1,128)} copy-done((f32[128,1,6272]{2,1,0:T(1,128)}, f32[128,1,6272]{2,1,0:T(1,128)S(1)}, u32[]{:S(2)}) %copy-start) | copy-done | bytes 3211288
  63.2 13.4 %shard_map.106 = (f32[8,256,256]{2,1,0:T(8,128)}, f32[3,8,8,128]{3,2,1,0:T(8,128)}, f32[3,8,8,128]{3,2,1,0:T(8,128)}, f32[3,8,4,256]{3,2,1,0:T(4,128)}, f32[3,8,4,256]{3,2,1,0:T(4,128)}) custom-call(s32[6]{0:T(128)} %convert_element_type.3.flag_ref, f32[6272,128]{1,0:T(8,128)} %bitcast.10, f32[2,8,8,128]{3,2,1,0:T(8,128)} %get-tuple-element.14.left_in, ...), custom_call_target="tpu_custom_call" | custom-call | tf_op jit(solution)/shard_map/pallas_call | solution.py:257
  76.6 2.2 %collective-permute-start = (f32[3,8,8,128]{3,2,1,0:T(8,128)}, f32[3,8,8,128]{3,2,1,0:T(8,128)S(1)}, u32[]{:S(2)}, u32[]{:S(2)}) collective-permute-start(f32[3,8,8,128]{3,2,1,0:T(8,128)} %get-tuple-element.20), channel_id=1, source_target_pairs={{0,1},{1,0},{2,3},{3,2},{4,5},{5,4},{6,7},{7,6},{8,9},{9,8},{10,11... | collective-permute-start | bytes 294920 | tf_op jit(solution)/shard_map/ppermute | solution.py:519
  78.8 1.3 %collective-permute-start.1 = (f32[3,8,8,128]{3,2,1,0:T(8,128)}, f32[3,8,8,128]{3,2,1,0:T(8,128)S(1)}, u32[]{:S(2)}, u32[]{:S(2)}) collective-permute-start(f32[3,8,8,128]{3,2,1,0:T(8,128)} %get-tuple-element.21), channel_id=1, source_target_pairs={{0,7},{1,2},{2,1},{3,4},{4,3},{5,6},{6,5},{7,0},{8,15},{9,10},{10,... | collective-permute-start | bytes 294920 | tf_op jit(solution)/shard_map/ppermute | solution.py:519
  80.2 3.0 %collective-permute-done.first_in.first_y = f32[3,8,8,128]{3,2,1,0:T(8,128)S(1)} collective-permute-done((f32[3,8,8,128]{3,2,1,0:T(8,128)}, f32[3,8,8,128]{3,2,1,0:T(8,128)S(1)}, u32[]{:S(2)}, u32[]{:S(2)}) %collective-permute-start) | collective-permute-done | bytes 98336 | tf_op jit(solution)/shard_map/ppermute | solution.py:519
  83.1 0.0 copy-start.1
  83.2 4.1 %collective-permute-done.1.second_in.second_y = f32[3,8,8,128]{3,2,1,0:T(8,128)S(1)} collective-permute-done((f32[3,8,8,128]{3,2,1,0:T(8,128)}, f32[3,8,8,128]{3,2,1,0:T(8,128)S(1)}, u32[]{:S(2)}, u32[]{:S(2)}) %collective-permute-start.1) | collective-permute-done | bytes 98336 | tf_op jit(solution)/shard_map/ppermute | solution.py:519
  87.3 0.0 copy-start.2
  87.3 0.0 copy-done.1
  87.3 0.6 copy-done.2
  87.9 1.9 %shard_map.107 = (f32[8,4,896]{2,1,0:T(4,128)}, f32[8,4,896]{2,1,0:T(4,128)}) custom-call(s32[6]{0:T(128)} %convert_element_type.3.flag_ref, f32[3,8,8,128]{3,2,1,0:T(8,128)} %copy-done.1, f32[3,8,8,128]{3,2,1,0:T(8,128)} %copy-done.2, f32[3,8,4,256]{3,2,1,0:T(4,128)} %get-tuple-element.22.low_in, f32[3,8,4,256]{3,2,1,0:T(4,128)} %get-tuple-element.23.high_in), custom_call_target="tpu_custom_call" | custom-call | tf_op jit(solution)/shard_map/pallas_call | solution.py:310
  89.8 0.0 collective-permute-start.2
  89.8 1.4 %collective-permute-start.3 = (f32[8,4,896]{2,1,0:T(4,128)}, f32[8,4,896]{2,1,0:T(4,128)S(1)}, u32[]{:S(2)}, u32[]{:S(2)}) collective-permute-start(f32[8,4,896]{2,1,0:T(4,128)} %get-tuple-element.25), channel_id=1, source_target_pairs={{0,120},{8,16},{16,8},{24,32},{32,24},{40,48},{48,40},{56,64},{64,... | collective-permute-start | bytes 344072 | tf_op jit(solution)/shard_map/ppermute | solution.py:519
  91.2 0.1 collective-permute-done.2.first_x
  91.3 0.0 copy-start.3
  91.3 5.0 %collective-permute-done.3.second_x = f32[8,4,896]{2,1,0:T(4,128)S(1)} collective-permute-done((f32[8,4,896]{2,1,0:T(4,128)}, f32[8,4,896]{2,1,0:T(4,128)S(1)}, u32[]{:S(2)}, u32[]{:S(2)}) %collective-permute-start.3) | collective-permute-done | bytes 114720 | tf_op jit(solution)/shard_map/ppermute | solution.py:519
  96.3 0.0 copy-start.4
  96.3 0.0 copy-done.3
  96.4 0.6 copy-done.4
  97.0 24.6 %shard_map.108 = f32[8,256,256]{2,1,0:T(8,128)} custom-call(s32[8]{0:T(128)} %kind_ref.3, f32[4]{0:T(128)} %slope_ref.1, s32[6]{0:T(128)} %convert_element_type.3.flag_ref, f32[8,256,256]{2,1,0:T(8,128)} %warmth_hbm.1, f32[8,256,256]{2,1,0:T(8,128)} %get-tuple-element.19.q_hbm, f32[8,256,256]{2,1,0:T(8,128)} %get-tuple-element.12.field_hbm, ...), custom_call_target="tpu_custom_call" | custom-call | tf_op jit(solution)/shard_map/pallas_call | solution.py:495
Async XLA Ops:
  9.0 52.5 %all-to-all-start = ((f32[128,1,6272]{2,1,0:T(1,128)}), f32[128,1,6272]{2,1,0:T(1,128)S(1)}, u32[]{:S(2)}, u32[]{:S(2)}) async-start(f32[128,1,6272]{2,1,0:T(1,128)} %bitcast.11), calls=%async_computation | async-start | bytes 6422528 | tf_op jit(solution)/shard_map/all_to_all | solution.py:540
  61.6 1.7 %copy-start = (f32[128,1,6272]{2,1,0:T(1,128)}, f32[128,1,6272]{2,1,0:T(1,128)S(1)}, u32[]{:S(2)}) copy-start(f32[128,1,6272]{2,1,0:T(1,128)S(1)} %all-to-all-done) | copy-start | bytes 9633796
  76.6 6.5 %collective-permute-start = (f32[3,8,8,128]{3,2,1,0:T(8,128)}, f32[3,8,8,128]{3,2,1,0:T(8,128)S(1)}, u32[]{:S(2)}, u32[]{:S(2)}) collective-permute-start(f32[3,8,8,128]{3,2,1,0:T(8,128)} %get-tuple-element.20), channel_id=1, source_target_pairs={{0,1},{1,0},{2,3},{3,2},{4,5},{5,4},{6,7},{7,6},{8,9},{9,8},{10,11... | collective-permute-start | bytes 294920 | tf_op jit(solution)/shard_map/ppermute | solution.py:519
  78.8 8.4 %collective-permute-start.1 = (f32[3,8,8,128]{3,2,1,0:T(8,128)}, f32[3,8,8,128]{3,2,1,0:T(8,128)S(1)}, u32[]{:S(2)}, u32[]{:S(2)}) collective-permute-start(f32[3,8,8,128]{3,2,1,0:T(8,128)} %get-tuple-element.21), channel_id=1, source_target_pairs={{0,7},{1,2},{2,1},{3,4},{4,3},{5,6},{6,5},{7,0},{8,15},{9,10},{10,... | collective-permute-start | bytes 294920 | tf_op jit(solution)/shard_map/ppermute | solution.py:519
  83.1 4.1 %copy-start.1 = (f32[3,8,8,128]{3,2,1,0:T(8,128)}, f32[3,8,8,128]{3,2,1,0:T(8,128)S(1)}, u32[]{:S(2)}) copy-start(f32[3,8,8,128]{3,2,1,0:T(8,128)S(1)} %collective-permute-done.first_in.first_y) | copy-start | bytes 294916
  87.3 0.6 copy-start.2
  89.8 1.5 %collective-permute-start.2 = (f32[8,4,896]{2,1,0:T(4,128)}, f32[8,4,896]{2,1,0:T(4,128)S(1)}, u32[]{:S(2)}, u32[]{:S(2)}) collective-permute-start(f32[8,4,896]{2,1,0:T(4,128)} %get-tuple-element.24), channel_id=1, source_target_pairs={{0,8},{8,0},{16,24},{24,16},{32,40},{40,32},{48,56},{56,48},{64,72... | collective-permute-start | bytes 344072 | tf_op jit(solution)/shard_map/ppermute | solution.py:519
  89.8 6.5 %collective-permute-start.3 = (f32[8,4,896]{2,1,0:T(4,128)}, f32[8,4,896]{2,1,0:T(4,128)S(1)}, u32[]{:S(2)}, u32[]{:S(2)}) collective-permute-start(f32[8,4,896]{2,1,0:T(4,128)} %get-tuple-element.25), channel_id=1, source_target_pairs={{0,120},{8,16},{16,8},{24,32},{32,24},{40,48},{48,40},{56,64},{64,... | collective-permute-start | bytes 344072 | tf_op jit(solution)/shard_map/ppermute | solution.py:519
  91.3 5.0 %copy-start.3 = (f32[8,4,896]{2,1,0:T(4,128)}, f32[8,4,896]{2,1,0:T(4,128)S(1)}, u32[]{:S(2)}) copy-start(f32[8,4,896]{2,1,0:T(4,128)S(1)} %collective-permute-done.2.first_x) | copy-start | bytes 344068
  96.3 0.6 copy-start.4

commit v2 on v1

--- a/solution.py
+++ b/solution.py
@@ -14,7 +14,7 @@
 NY = 256
 GROUPS = NX // 8
 POSITIONS = LAYERS * NX * NY // RUN
-ACCS = 8
+ACCS = 6
 WALL = 1e30
 BASE = 16
 ROWS = 280
@@ -162,41 +162,29 @@
         ),
         in_specs=[smem, smem, vmem, vmem],
         out_specs=(vmem,) * 5,
-        compiler_params=pltpu.CompilerParams(vmem_limit_bytes=VMEM_LIMIT),
+        compiler_params=pltpu.CompilerParams(vmem_limit_bytes=16 * 1024 * 1024),
         cost_estimate=pl.CostEstimate(flops=8000000, bytes_accessed=6300000, transcendentals=0),
     )(kind, base, warmth, scale)
 
 
 def gather_kernel(
-    flag_ref, inc_hbm, left_in, right_in, low_in, high_in,
-    field_hbm, first_ref, second_ref, low_ref, high_ref,
-    inc_ref, field_ref, spot_v, spot_s, inc_sem, spot_sem, field_sem, *accs,
+    flag_ref, inc_ref, left_in, right_in, low_in, high_in,
+    field_hbm, first_hbm, second_hbm, low_ref, high_ref,
+    first_ref, second_ref, field_ref, spot_v, spot_s, spot_sem, field_sem, side_sem, *accs,
 ):
     tiles = 128
-    parts = 8
-    size = tiles * CHUNK // parts
-    loads = [
-        pltpu.make_async_copy(
-            inc_hbm.at[pl.ds(i * size, size), :], inc_ref.at[pl.ds(i * size, size), :], inc_sem.at[i]
-        )
-        for i in range(parts)
-    ]
-    for c in loads:
-        c.start()
-
-    def clear(i, _):
-        for acc in accs:
-            acc[pl.ds(pl.multiple_of(i * 64, 64), 64), :] = jnp.zeros((64, RUN), F32)
-        return 0
-
-    lax.fori_loop(0, POSITIONS // 64, clear, 0)
-    for c in loads:
-        c.wait()
     for t in range(tiles):
         row = inc_ref[t * CHUNK + CAP : t * CHUNK + CAP + 1, :]
         spot_v[t : t + 1, :] = jnp.where(row > 0.5, row.astype(jnp.int32) - 1, POSITIONS)
     copy = pltpu.make_async_copy(spot_v, spot_s, spot_sem)
     copy.start()
+
+    def clear(i, _):
+        for acc in accs:
+            acc[pl.ds(pl.multiple_of(i * 64, 64), 64), :] = jnp.zeros((64, RUN), F32)
+        return 0
+
+    lax.fori_loop(0, POSITIONS // 64, clear, 0)
     copy.wait()
 
     def source(s, _):
@@ -228,10 +216,8 @@
             for h in range(2):
                 cols = slice(h * RUN, (h + 1) * RUN)
                 start = pl.multiple_of(l * 512 + g * 16 + h * 8, 8)
-                terms = [acc[pl.ds(start, 8), :] for acc in accs]
-                while len(terms) > 1:
-                    terms = [sum(terms[i : i + 2]) for i in range(0, len(terms), 2)]
-                total = terms[0]
+                v = [acc[pl.ds(start, 8), :] for acc in accs]
+                total = ((v[0] + v[1]) + (v[2] + v[3])) + (v[4] + v[5])
                 field_ref[l, 8 * g : 8 * g + 8, cols] = total
                 if h == 0:
                     sides[0] = fold_left(sides[0], total, g, slot)
@@ -246,13 +232,21 @@
         return 0
 
     lax.fori_loop(0, LAYERS, layer, 0)
+    sides = [
+        pltpu.make_async_copy(first_ref, first_hbm, side_sem.at[0]),
+        pltpu.make_async_copy(second_ref, second_hbm, side_sem.at[1]),
+    ]
+    for c in sides:
+        c.start()
     for l in range(LAYERS):
         stored(l).wait()
+    for c in sides:
+        c.wait()
 
 
 def gather(flags, incoming, left, right, low, high):
     vmem = pl.BlockSpec(memory_space=pltpu.VMEM)
-    hbm = pl.BlockSpec(memory_space=pl.ANY)
+    hbm = pl.BlockSpec(memory_space=pltpu.HBM)
     smem = pl.BlockSpec(memory_space=pltpu.SMEM)
     return pl.pallas_call(
         gather_kernel,
@@ -263,23 +257,26 @@
             jax.ShapeDtypeStruct((3, LAYERS, 4, NY), F32),
             jax.ShapeDtypeStruct((3, LAYERS, 4, NY), F32),
         ),
-        in_specs=[smem, hbm] + [vmem] * 4,
-        out_specs=(hbm,) + (vmem,) * 4,
+        in_specs=[smem] + [vmem] * 5,
+        out_specs=(hbm,) * 3 + (vmem,) * 2,
         scratch_shapes=[
-            pltpu.VMEM((128 * CHUNK, RUN), F32),
+            pltpu.VMEM((3, LAYERS, 8, RUN), F32),
+            pltpu.VMEM((3, LAYERS, 8, RUN), F32),
             pltpu.VMEM((LAYERS, NX, NY), F32),
             pltpu.VMEM((128, RUN), jnp.int32),
             pltpu.SMEM((128, RUN), jnp.int32),
-            pltpu.SemaphoreType.DMA((8,)),
             pltpu.SemaphoreType.DMA,
             pltpu.SemaphoreType.DMA((LAYERS,)),
+            pltpu.SemaphoreType.DMA((2,)),
         ]
         + [pltpu.VMEM((POSITIONS + 8, RUN), F32)] * ACCS,
-        compiler_params=pltpu.CompilerParams(vmem_limit_bytes=VMEM_LIMIT),
+        compiler_params=pltpu.CompilerParams(vmem_limit_bytes=24 * 1024 * 1024),
     )(flags, incoming, left, right, low, high)
 
 
-def corner_kernel(flag_ref, first_in, second_in, low_in, high_in, first_ref, second_ref):
+def corner_kernel(
+    flag_ref, first_in, second_in, low_in, high_in, first_hbm, second_hbm, first_ref, second_ref, sem
+):
     slot = iota((8, RUN), 1) // 4
     even_y = flag_ref[4] > 0
     even_x = flag_ref[5] > 0
@@ -301,6 +298,14 @@
                 high = jnp.where(slot == k, pltpu.roll(v, (4 * k + 4) % RUN, 1), high)
             send(l, slice(q * NY, (q + 1) * NY), low_in[q, l], high_in[q, l])
         send(l, slice(3 * NY, 3 * NY + RUN), low[:4], high[4:])
+    sides = [
+        pltpu.make_async_copy(first_ref, first_hbm, sem.at[0]),
+        pltpu.make_async_copy(second_ref, second_hbm, sem.at[1]),
+    ]
+    for c in sides:
+        c.start()
+    for c in sides:
+        c.wait()
 
 
 def corners(flags, first, second, low, high):
@@ -311,7 +316,9 @@
         corner_kernel,
         out_shape=(shape, shape),
         in_specs=[smem] + [vmem] * 4,
-        out_specs=(vmem,) * 2,
+        out_specs=(pl.BlockSpec(memory_space=pltpu.HBM),) * 2,
+        scratch_shapes=[pltpu.VMEM(shape.shape, F32)] * 2 + [pltpu.SemaphoreType.DMA((2,))],
+        compiler_params=pltpu.CompilerParams(vmem_limit_bytes=4 * 1024 * 1024),
     )(flags, first, second, low, high)
 
 
@@ -489,7 +496,7 @@
 def sweeps(kind, slope, flags, warmth, q, field, first_y, second_y, first_x, second_x):
     vmem = pl.BlockSpec(memory_space=pltpu.VMEM)
     smem = pl.BlockSpec(memory_space=pltpu.SMEM)
-    hbm = pl.BlockSpec(memory_space=pl.ANY)
+    hbm = pl.BlockSpec(memory_space=pltpu.HBM)
     ext = pltpu.VMEM((LAYERS, 3, ROWS, RUN), F32)
     row = pltpu.VMEM((LAYERS, 3, 8, RUN), F32)
     return pl.pallas_call(
@@ -508,7 +515,7 @@
             pltpu.VMEM((4, LAYERS, 3, 8, RUN), F32),
             pltpu.SemaphoreType.DMA((3, LAYERS, 2)),
         ],
-        compiler_params=pltpu.CompilerParams(vmem_limit_bytes=VMEM_LIMIT),
+        compiler_params=pltpu.CompilerParams(vmem_limit_bytes=64 * 1024 * 1024 - 1600 * 1024),
     )(kind, slope, flags, warmth, q, field, first_y, second_y, first_x, second_x)
 
 

time: 122 us -> 116 us (0.951)
  Pallas kernels: 52.9 us -> 45.2 us
  local copies, waits for them, and re-layouts: 3.05 us -> 5.28 us
  starting transfers between devices: 16.1 us -> 17.7 us
  waiting for transfers between devices: 47.7 us -> 46.3 us
    pallas_call x1, Pallas kernels: 5.25 us -> 2.22 us  [prepare(): pl.pallas_call(prepare_kernel, out_shape=(jax.ShapeDtypeStruct(warmth.sha...]
    pallas_call x1, Pallas kernels: 13.4 us -> 10.8 us  [gather(): pl.pallas_call(gather_kernel, out_shape=(jax.ShapeDtypeStruct((LAYERS, NX...]
    unnamed x10 -> x20, local copies, waits for them, and re-layouts: 2.95 us -> 5.18 us
    all_to_all x1, starting transfers between devices: 11.1 us -> 12.6 us  [per_device(): lax.all_to_all(outgoing.reshape(tiles, 1, CHUNK * RUN), ('gx', 'gy'), spl...]
  transfers between devices with their start and end apart: 5 -> 5, of which waited for: 5 -> 4; matrix products, arithmetic and copies ran while one was open for 1% -> 0% of each run, Pallas kernels for 4% -> 2%
where the time goes in v2:
time: 116 us
  waiting for transfers between devices  46.3 us (40%)
  Pallas kernels  45.2 us (39%)
  starting transfers between devices  17.7 us (15%)
  local copies, waits for them, and re-layouts  5.28 us (5%)
  between operations  1.4 us (1%)
    all_to_all x1, waiting for transfers between devices, per_device(): lax.all_to_all(outgoing.reshape(tiles, 1, CHUNK * RUN), ('gx', 'gy'), spl...  34.5 us
    pallas_call x1, Pallas kernels, sweeps(): pl.pallas_call(sweep_kernel, out_shape=jax.ShapeDtypeStruct((LAYERS, NX,...  24.6 us
    all_to_all x1, starting transfers between devices, per_device(): lax.all_to_all(outgoing.reshape(tiles, 1, CHUNK * RUN), ('gx', 'gy'), spl...  12.6 us
    pallas_call x1, Pallas kernels, gather(): pl.pallas_call(gather_kernel, out_shape=(jax.ShapeDtypeStruct((LAYERS, NX...  10.8 us
    ppermute x2, waiting for transfers between devices, swap(): lax.ppermute(second, axis, others)  9.1 us
    pallas_call x1, Pallas kernels, pack(): pl.pallas_call(pack_kernel, out_shape=jax.ShapeDtypeStruct((tiles * CHUNK...  6.58 us
    unnamed x20, local copies, waits for them, and re-layouts  5.18 us
    ppermute x2, starting transfers between devices, swap(): lax.ppermute(second, axis, others)  2.77 us
  transfers between devices with their start and end apart: 5, of which 4 were waited for; matrix products, arithmetic and copies ran while one was open for 0% of the time, Pallas kernels for 2%

profile of v2, /device:TPU:0, one launch (start us, length us, event | category | flops | bytes accessed | tf_op | source)
XLA Modules:
  0.0 115.9 jit_solution(1361844599784039582)
XLA Ops:
  1.3 6.6 %shard_map.104 = f32[6272,128]{1,0:T(8,128)} custom-call(s32[1]{0:T(128)S(6)} %copy.12.tally_ref, s32[32,128]{1,0:T(8,128)} %bitcast.12, s32[32,128]{1,0:T(8,128)} %bitcast.13, f32[4096,128]{1,0:T(8,128)} %table_hbm.1), custom_call_target="tpu_custom_call" | custom-call | tf_op jit(solution)/shard_map/pallas_call | solution.py:87
  7.9 0.0 copy-start.6
  7.9 0.0 copy-start.7
  7.9 12.6 %all-to-all-start = ((f32[128,1,6272]{2,1,0:T(1,128)}), f32[128,1,6272]{2,1,0:T(1,128)S(1)}, u32[]{:S(2)}, u32[]{:S(2)}) async-start(f32[128,1,6272]{2,1,0:T(1,128)} %bitcast.11), calls=%async_computation | async-start | bytes 6422528 | tf_op jit(solution)/shard_map/all_to_all | solution.py:547
  20.5 0.1 stack.27
  20.7 0.0 copy-done.6
  20.7 0.0 copy-done.7
  20.7 0.0 copy-start
  20.7 1.6 %copy-done = f32[8,256,256]{2,1,0:T(8,128)S(1)} copy-done((f32[8,256,256]{2,1,0:T(8,128)S(1)}, f32[8,256,256]{2,1,0:T(8,128)}, u32[]{:S(2)}) %copy-start) | copy-done | bytes 2097176
  22.3 0.0 copy-start.2
  22.3 1.6 %copy-done.2 = f32[8,256,256]{2,1,0:T(8,128)S(1)} copy-done((f32[8,256,256]{2,1,0:T(8,128)S(1)}, f32[8,256,256]{2,1,0:T(8,128)}, u32[]{:S(2)}) %copy-start.2) | copy-done | bytes 2097176
  23.9 0.0 copy-start.5
  23.9 2.2 %shard_map.105 = (f32[8,256,256]{2,1,0:T(8,128)S(1)}, f32[2,8,8,128]{3,2,1,0:T(8,128)S(1)}, f32[2,8,8,128]{3,2,1,0:T(8,128)S(1)}, f32[2,8,4,256]{3,2,1,0:T(4,128)S(1)}, f32[2,8,4,256]{3,2,1,0:T(4,128)S(1)}) custom-call(s32[8]{0:T(128)S(1)} %copy-done.6, f32[4]{0:T(128)S(1)} %copy-done.7, f32[8,256,256]{2,1,0:T(8,128)S(1)} %copy-done, ...), custom_call_target="tpu_custom_call" | custom-call | flops 8000000 | bytes 6300000 | tf_op jit(solution)/shard_map/pallas_call | solution.py:154
  26.1 0.0 copy-start.1
  26.1 1.3 %copy-done.1 = f32[8,256,256]{2,1,0:T(8,128)} copy-done((f32[8,256,256]{2,1,0:T(8,128)}, f32[8,256,256]{2,1,0:T(8,128)S(1)}, u32[]{:S(2)}) %copy-start.1) | copy-done | bytes 2097176
  27.4 34.5 %all-to-all-done = f32[128,1,6272]{2,1,0:T(1,128)S(1)} async-done(((f32[128,1,6272]{2,1,0:T(1,128)}), f32[128,1,6272]{2,1,0:T(1,128)S(1)}, u32[]{:S(2)}, u32[]{:S(2)}) %all-to-all-start) | async-done | bytes 3211296 | tf_op jit(solution)/shard_map/all_to_all | solution.py:547
  61.9 10.8 %shard_map.106 = (f32[8,256,256]{2,1,0:T(8,128)}, f32[3,8,8,128]{3,2,1,0:T(8,128)S(1)}, f32[3,8,8,128]{3,2,1,0:T(8,128)S(1)}, f32[3,8,4,256]{3,2,1,0:T(4,128)S(1)}, f32[3,8,4,256]{3,2,1,0:T(4,128)S(1)}) custom-call(s32[6]{0:T(128)S(1)} %convert_element_type.3.flag_ref, f32[6272,128]{1,0:T(8,128)S(1)} %bitcast.10, ...), custom_call_target="tpu_custom_call" | custom-call | tf_op jit(solution)/shard_map/pallas_call | solution.py:251
  72.7 2.2 %collective-permute-start = (f32[3,8,8,128]{3,2,1,0:T(8,128)S(1)}, f32[3,8,8,128]{3,2,1,0:T(8,128)S(1)}, u32[]{:S(2)}, u32[]{:S(2)}) collective-permute-start(f32[3,8,8,128]{3,2,1,0:T(8,128)S(1)} %get-tuple-element.20), channel_id=1, source_target_pairs={{0,1},{1,0},{2,3},{3,2},{4,5},{5,4},{6,7},{7,6},{8,9},{9,8},{10,11... | collective-permute-start | bytes 294920 | tf_op jit(solution)/shard_map/ppermute | solution.py:526
  74.9 1.3 %collective-permute-start.1 = (f32[3,8,8,128]{3,2,1,0:T(8,128)S(1)}, f32[3,8,8,128]{3,2,1,0:T(8,128)S(1)}, u32[]{:S(2)}, u32[]{:S(2)}) collective-permute-start(f32[3,8,8,128]{3,2,1,0:T(8,128)S(1)} %get-tuple-element.21), channel_id=1, source_target_pairs={{0,7},{1,2},{2,1},{3,4},{4,3},{5,6},{6,5},{7,0},{8,15},{9,10},{10,... | collective-permute-start | bytes 294920 | tf_op jit(solution)/shard_map/ppermute | solution.py:526
  76.3 2.8 %collective-permute-done.first_in.first_y = f32[3,8,8,128]{3,2,1,0:T(8,128)S(1)} collective-permute-done((f32[3,8,8,128]{3,2,1,0:T(8,128)S(1)}, f32[3,8,8,128]{3,2,1,0:T(8,128)S(1)}, u32[]{:S(2)}, u32[]{:S(2)}) %collective-permute-start) | collective-permute-done | bytes 98336 | tf_op jit(solution)/shard_map/ppermute | solution.py:526
  79.0 0.0 copy-start.3
  79.0 4.1 %collective-permute-done.1.second_in.second_y = f32[3,8,8,128]{3,2,1,0:T(8,128)S(1)} collective-permute-done((f32[3,8,8,128]{3,2,1,0:T(8,128)S(1)}, f32[3,8,8,128]{3,2,1,0:T(8,128)S(1)}, u32[]{:S(2)}, u32[]{:S(2)}) %collective-permute-start.1) | collective-permute-done | bytes 98336 | tf_op jit(solution)/shard_map/ppermute | solution.py:526
  83.2 0.0 copy-start.4
  83.2 0.0 copy-done.5
  83.2 1.0 shard_map.107
  84.2 0.1 collective-permute-start.2
  84.3 1.4 %collective-permute-start.3 = (f32[8,4,896]{2,1,0:T(4,128)S(1)}, f32[8,4,896]{2,1,0:T(4,128)S(1)}, u32[]{:S(2)}, u32[]{:S(2)}) collective-permute-start(f32[8,4,896]{2,1,0:T(4,128)S(1)} %get-tuple-element.25), channel_id=1, source_target_pairs={{0,120},{8,16},{16,8},{24,32},{32,24},{40,48},{48,40},{56,64},{64,... | collective-permute-start | bytes 344072 | tf_op jit(solution)/shard_map/ppermute | solution.py:526
  85.7 0.0 collective-permute-done.2.first_x
  85.7 0.0 copy-start.8
  85.7 5.0 %collective-permute-done.3.second_x = f32[8,4,896]{2,1,0:T(4,128)S(1)} collective-permute-done((f32[8,4,896]{2,1,0:T(4,128)S(1)}, f32[8,4,896]{2,1,0:T(4,128)S(1)}, u32[]{:S(2)}, u32[]{:S(2)}) %collective-permute-start.3) | collective-permute-done | bytes 114720 | tf_op jit(solution)/shard_map/ppermute | solution.py:526
  90.7 0.0 copy-start.9
  90.7 0.0 copy-done.3
  90.7 0.0 copy-done.4
  90.7 0.0 copy-done.8
  90.7 0.6 copy-done.9
  91.3 24.6 %shard_map.108 = f32[8,256,256]{2,1,0:T(8,128)} custom-call(s32[8]{0:T(128)} %kind_ref.3, f32[4]{0:T(128)} %slope_ref.1, s32[6]{0:T(128)} %copy-done.5, f32[8,256,256]{2,1,0:T(8,128)} %warmth_hbm.1, f32[8,256,256]{2,1,0:T(8,128)} %copy-done.1, f32[8,256,256]{2,1,0:T(8,128)} %get-tuple-element.12.field_hbm, f32[3,8,8,128]{3,2,1,0:T(8,128)} %copy-done.3, ...), custom_call_target="tpu_custom_call" | custom-call | tf_op jit(solution)/shard_map/pallas_call | solution.py:502
  (1 shorter events, 0.0 us)
Async XLA Ops:
  7.9 12.8 %copy-start.6 = (s32[8]{0:T(128)S(1)}, s32[8]{0:T(128)}, u32[]{:S(2)}) copy-start(s32[8]{0:T(128)} %kind_ref.3) | copy-start | bytes 100
  7.9 12.8 %copy-start.7 = (f32[4]{0:T(128)S(1)}, f32[4]{0:T(128)}, u32[]{:S(2)}) copy-start(f32[4]{0:T(128)} %base_ref.1) | copy-start | bytes 52
  7.9 54.0 %all-to-all-start = ((f32[128,1,6272]{2,1,0:T(1,128)}), f32[128,1,6272]{2,1,0:T(1,128)S(1)}, u32[]{:S(2)}, u32[]{:S(2)}) async-start(f32[128,1,6272]{2,1,0:T(1,128)} %bitcast.11), calls=%async_computation | async-start | bytes 6422528 | tf_op jit(solution)/shard_map/all_to_all | solution.py:547
  20.7 1.6 %copy-start = (f32[8,256,256]{2,1,0:T(8,128)S(1)}, f32[8,256,256]{2,1,0:T(8,128)}, u32[]{:S(2)}) copy-start(f32[8,256,256]{2,1,0:T(8,128)} %warmth_hbm.1) | copy-start | bytes 6291460
  22.3 1.6 %copy-start.2 = (f32[8,256,256]{2,1,0:T(8,128)S(1)}, f32[8,256,256]{2,1,0:T(8,128)}, u32[]{:S(2)}) copy-start(f32[8,256,256]{2,1,0:T(8,128)} %scale_ref.1) | copy-start | bytes 6291460
  23.9 59.3 %copy-start.5 = (s32[6]{0:T(128)}, s32[6]{0:T(128)S(1)}, u32[]{:S(2)}) copy-start(s32[6]{0:T(128)S(1)} %convert_element_type.3.flag_ref) | copy-start | bytes 76
  26.1 1.4 %copy-start.1 = (f32[8,256,256]{2,1,0:T(8,128)}, f32[8,256,256]{2,1,0:T(8,128)S(1)}, u32[]{:S(2)}) copy-start(f32[8,256,256]{2,1,0:T(8,128)S(1)} %get-tuple-element.19.q_hbm) | copy-start | bytes 6291460
  72.7 6.3 %collective-permute-start = (f32[3,8,8,128]{3,2,1,0:T(8,128)S(1)}, f32[3,8,8,128]{3,2,1,0:T(8,128)S(1)}, u32[]{:S(2)}, u32[]{:S(2)}) collective-permute-start(f32[3,8,8,128]{3,2,1,0:T(8,128)S(1)} %get-tuple-element.20), channel_id=1, source_target_pairs={{0,1},{1,0},{2,3},{3,2},{4,5},{5,4},{6,7},{7,6},{8,9},{9,8},{10,11... | collective-permute-start | bytes 294920 | tf_op jit(solution)/shard_map/ppermute | solution.py:526
  74.9 8.2 %collective-permute-start.1 = (f32[3,8,8,128]{3,2,1,0:T(8,128)S(1)}, f32[3,8,8,128]{3,2,1,0:T(8,128)S(1)}, u32[]{:S(2)}, u32[]{:S(2)}) collective-permute-start(f32[3,8,8,128]{3,2,1,0:T(8,128)S(1)} %get-tuple-element.21), channel_id=1, source_target_pairs={{0,7},{1,2},{2,1},{3,4},{4,3},{5,6},{6,5},{7,0},{8,15},{9,10},{10,... | collective-permute-start | bytes 294920 | tf_op jit(solution)/shard_map/ppermute | solution.py:526
  79.0 11.7 %copy-start.3 = (f32[3,8,8,128]{3,2,1,0:T(8,128)}, f32[3,8,8,128]{3,2,1,0:T(8,128)S(1)}, u32[]{:S(2)}) copy-start(f32[3,8,8,128]{3,2,1,0:T(8,128)S(1)} %collective-permute-done.first_in.first_y) | copy-start | bytes 294916
  83.2 7.5 %copy-start.4 = (f32[3,8,8,128]{3,2,1,0:T(8,128)}, f32[3,8,8,128]{3,2,1,0:T(8,128)S(1)}, u32[]{:S(2)}) copy-start(f32[3,8,8,128]{3,2,1,0:T(8,128)S(1)} %collective-permute-done.1.second_in.second_y) | copy-start | bytes 294916
  84.2 1.5 %collective-permute-start.2 = (f32[8,4,896]{2,1,0:T(4,128)S(1)}, f32[8,4,896]{2,1,0:T(4,128)S(1)}, u32[]{:S(2)}, u32[]{:S(2)}) collective-permute-start(f32[8,4,896]{2,1,0:T(4,128)S(1)} %get-tuple-element.24), channel_id=1, source_target_pairs={{0,8},{8,0},{16,24},{24,16},{32,40},{40,32},{48,56},{56,48},{64,72... | collective-permute-start | bytes 344072 | tf_op jit(solution)/shard_map/ppermute | solution.py:526
  84.3 6.4 %collective-permute-start.3 = (f32[8,4,896]{2,1,0:T(4,128)S(1)}, f32[8,4,896]{2,1,0:T(4,128)S(1)}, u32[]{:S(2)}, u32[]{:S(2)}) collective-permute-start(f32[8,4,896]{2,1,0:T(4,128)S(1)} %get-tuple-element.25), channel_id=1, source_target_pairs={{0,120},{8,16},{16,8},{24,32},{32,24},{40,48},{48,40},{56,64},{64,... | collective-permute-start | bytes 344072 | tf_op jit(solution)/shard_map/ppermute | solution.py:526
  85.7 5.0 %copy-start.8 = (f32[8,4,896]{2,1,0:T(4,128)}, f32[8,4,896]{2,1,0:T(4,128)S(1)}, u32[]{:S(2)}) copy-start(f32[8,4,896]{2,1,0:T(4,128)S(1)} %collective-permute-done.2.first_x) | copy-start | bytes 344068
  90.7 0.6 copy-start.9

commit v3 on v2

v3 whole, which is shorter than its diff:
```python
import jax
import jax.numpy as jnp
from jax import lax
from jax.experimental import pallas as pl
from jax.experimental.pallas import tpu as pltpu
from jax.sharding import PartitionSpec as P

RUN = 128
SWEEPS = 3
CAP = 48
CHUNK = CAP + 1
LAYERS = 8
NX = 256
NY = 256
GROUPS = NX // 8
POSITIONS = LAYERS * NX * NY // RUN
ACCS = 6
FIELDS = ((0, 3), (3, 3), (6, 2))
WALL = 1e30
SINK = 4.0
BASE = 16
ROWS = 280
VMEM_LIMIT = 60 * 1024 * 1024
F32 = jnp.float32
BF16 = jnp.bfloat16


def iota(shape, dim):
    return lax.broadcasted_iota(jnp.int32, shape, dim)


def pack_kernel(
    tally_ref, target_ref, place_ref, table_hbm, out_ref, table_ref, dest_v, dest_s, sem, table_sem
):
    load = pltpu.make_async_copy(table_hbm, table_ref, table_sem)
    load.start()
    tally = tally_ref[0]
    tiles = 128
    sub = iota((tiles, RUN), 0)
    lane = iota((1, RUN), 1)
    tri_row = iota((RUN, 2 * RUN), 0)
    tri_col = iota((RUN, 2 * RUN), 1)
    tri = jnp.where((tri_row <= tri_col) | (tri_col >= RUN), 1.0, 0.0).astype(BF16)

    def rank_group(g, carry):
        seen, placed = carry
        live = (lane + g * RUN) < tally
        tgt = target_ref[pl.ds(g, 1), :]
        match = sub == jnp.where(live, tgt, -1)
        onehot = jnp.where(match, 1.0, 0.0)
        run = jnp.dot(onehot.astype(BF16), tri, preferred_element_type=F32)
        rank = jnp.sum(jnp.where(match, seen + run[:, :RUN], 0.0), axis=0, keepdims=True)
        rank = rank.astype(jnp.int32) - 1
        dest_v[pl.ds(g, 1), :] = jnp.where(live, tgt * CHUNK + rank, CAP)
        spot = place_ref[pl.ds(g, 1), :]
        spot = (spot & ~15) | ((spot & 1) << 3) | ((spot >> 1) & 7)
        spot = spot + 1
        digits = jnp.where(sub < 64, spot & 63, spot >> 6)
        chosen = jnp.where((sub & 63) == rank, digits, 0).astype(F32)
        placed = placed + lax.dot_general(
            onehot.astype(BF16),
            chosen.astype(BF16),
            (((1,), (1,)), ((), ())),
            preferred_element_type=F32,
        )
        return seen + run[:, RUN:], placed

    zero = jnp.zeros((tiles, RUN), F32)
    seen, placed = lax.fori_loop(0, 32, rank_group, (zero, zero), unroll=32)
    placed = placed + 64.0 * pltpu.roll(placed, 64, 1)
    copy = pltpu.make_async_copy(dest_v, dest_s, sem)
    copy.start()
    copy.wait()

    load.wait()

    def move(g, _):
        for k in range(RUN):
            out_ref[pl.ds(dest_s[g, k], 1), :] = table_ref[pl.ds(g * RUN + k, 1), :]
        return 0

    lax.fori_loop(0, (tally + RUN - 1) // RUN, move, 0)
    for t in range(tiles):
        out_ref[t * CHUNK + CAP : t * CHUNK + CAP + 1, :] = placed[t : t + 1, :]


def pack(tally, target, place, table):
    tiles = 128
    return pl.pallas_call(
        pack_kernel,
        out_shape=jax.ShapeDtypeStruct((tiles * CHUNK, RUN), F32),
        in_specs=[
            pl.BlockSpec(memory_space=pltpu.SMEM),
            pl.BlockSpec(memory_space=pltpu.VMEM),
            pl.BlockSpec(memory_space=pltpu.VMEM),
            pl.BlockSpec(memory_space=pl.ANY),
        ],
        out_specs=pl.BlockSpec(memory_space=pltpu.VMEM),
        scratch_shapes=[
            pltpu.VMEM((32 * RUN, RUN), F32),
            pltpu.VMEM((32, RUN), jnp.int32),
            pltpu.SMEM((32, RUN), jnp.int32),
            pltpu.SemaphoreType.DMA,
            pltpu.SemaphoreType.DMA,
        ],
        compiler_params=pltpu.CompilerParams(vmem_limit_bytes=VMEM_LIMIT),
    )(tally, target, place, table)


def fold(kept, value, shift, slot, g):
    return jnp.where(slot == g, pltpu.roll(value, shift % RUN, 1), kept)


def prepare_kernel(
    kind_ref, base_ref, slope_ref, warmth_ref, scale_ref, q_ref, left_ref, right_ref, low_ref, high_ref
):
    lane = iota((8, RUN), 1)
    slot = lane // 8
    use_q = lane % 8 >= 3
    sub = iota((8, RUN), 0)

    def layer(l, _):
        kind = kind_ref[l]
        ratio = jnp.full((8, RUN), 0.5 * slope_ref[kind], F32) / jnp.full((8, RUN), base_ref[kind], F32)
        zero = jnp.zeros((8, RUN), F32)
        left = [[zero, zero], [zero, zero]]
        right = [[zero, zero], [zero, zero]]
        for g in range(GROUPS):
            half = g // 16
            k = g % 16
            for h in range(2):
                cols = slice(h * RUN, (h + 1) * RUN)
                t = warmth_ref[l, 8 * g : 8 * g + 8, cols]
                q = ratio / scale_ref[l, 8 * g : 8 * g + 8, cols]
                q_ref[l, 8 * g : 8 * g + 8, cols] = q
                if h == 0:
                    left[half][0] = fold(left[half][0], t, 8 * k, slot, k)
                    left[half][1] = fold(left[half][1], q, 8 * k + 3, slot, k)
                else:
                    right[half][0] = fold(right[half][0], t, 8 * k + 3, slot, k)
                    right[half][1] = fold(right[half][1], q, 8 * k + 6, slot, k)
                if g == 0:
                    low_ref[l, :, cols] = jnp.where(sub < 3, t, pltpu.roll(q, 3, 0))
                if g == GROUPS - 1:
                    high_ref[l, :, cols] = jnp.where(sub < 3, pltpu.roll(t, 3, 0), pltpu.roll(q, 6, 0))
        for half in range(2):
            left_ref[l, half] = jnp.where(use_q, left[half][1], left[half][0])
            right_ref[l, half] = jnp.where(use_q, right[half][1], right[half][0])
        return 0

    lax.fori_loop(0, LAYERS, layer, 0)


def prepare(kind, base, slope, warmth, scale):
    vmem = pl.BlockSpec(memory_space=pltpu.VMEM)
    smem = pl.BlockSpec(memory_space=pltpu.SMEM)
    side = jax.ShapeDtypeStruct((LAYERS, 2, 8, RUN), F32)
    edge = jax.ShapeDtypeStruct((LAYERS, 8, NY), F32)
    return pl.pallas_call(
        prepare_kernel,
        out_shape=(jax.ShapeDtypeStruct(warmth.shape, F32), side, side, edge, edge),
        in_specs=[smem, smem, smem, vmem, vmem],
        out_specs=(vmem,) * 5,
        compiler_params=pltpu.CompilerParams(vmem_limit_bytes=16 * 1024 * 1024),
        cost_estimate=pl.CostEstimate(flops=8000000, bytes_accessed=6300000, transcendentals=0),
    )(kind, base, slope, warmth, scale)


def gather_kernel(
    flag_ref, inc_ref, left_in, right_in, low_in, high_in,
    field_hbm, first_hbm, second_hbm, low_ref, high_ref,
    first_ref, second_ref, field_ref, spot_v, spot_s, spot_sem, field_sem, side_sem, *accs,
):
    tiles = 128
    for t in range(tiles):
        row = inc_ref[t * CHUNK + CAP : t * CHUNK + CAP + 1, :]
        spot_v[t : t + 1, :] = jnp.where(row > 0.5, row.astype(jnp.int32) - 1, POSITIONS)
    copy = pltpu.make_async_copy(spot_v, spot_s, spot_sem)
    copy.start()

    def clear(i, _):
        for acc in accs:
            acc[pl.ds(pl.multiple_of(i * 64, 64), 64), :] = jnp.zeros((64, RUN), F32)
        return 0

    lax.fori_loop(0, POSITIONS // 64, clear, 0)
    copy.wait()

    def source(s, _):
        for p in range(CAP):
            acc = accs[p % ACCS]
            acc[pl.ds(spot_s[s, p], 1), :] += inc_ref[pl.ds(s * CHUNK + p, 1), :]
        return 0

    lax.fori_loop(0, tiles, source, 0)
    even = flag_ref[4] > 0
    lane = iota((8, RUN), 1)
    slot = lane // 8
    use_p = lane % 8 >= 6
    sub = iota((8, RUN), 0)

    def stored(l):
        return pltpu.make_async_copy(field_ref.at[l], field_hbm.at[l], field_sem.at[l])

    def layer(l, _):
        zero = jnp.zeros((8, RUN), F32)
        left = [zero, zero]
        right = [zero, zero]
        for g in range(GROUPS):
            half = g // 16
            k = g % 16
            for h in range(2):
                cols = slice(h * RUN, (h + 1) * RUN)
                start = pl.multiple_of(l * 512 + g * 16 + h * 8, 8)
                v = [acc[pl.ds(start, 8), :] for acc in accs]
                total = ((v[0] + v[1]) + (v[2] + v[3])) + (v[4] + v[5])
                field_ref[l, 8 * g : 8 * g + 8, cols] = total
                if h == 0:
                    left[half] = fold(left[half], total, 8 * k + 6, slot, k)
                else:
                    right[half] = fold(right[half], total, 8 * k + 8, slot, k)
                if g == 0:
                    low_ref[l, :, cols] = jnp.where(sub < 6, low_in[l, :, cols], pltpu.roll(total, 6, 0))
                if g == GROUPS - 1:
                    high_ref[l, :, cols] = jnp.where(sub < 6, high_in[l, :, cols], total)
        for half in range(2):
            lhs = jnp.where(use_p, left[half], left_in[l, half])
            rhs = jnp.where(use_p, right[half], right_in[l, half])
            first_ref[l, half] = jnp.where(even, rhs, lhs)
            second_ref[l, half] = jnp.where(even, lhs, rhs)
        stored(l).start()
        return 0

    lax.fori_loop(0, LAYERS, layer, 0)
    sides = [
        pltpu.make_async_copy(first_ref, first_hbm, side_sem.at[0]),
        pltpu.make_async_copy(second_ref, second_hbm, side_sem.at[1]),
    ]
    for c in sides:
        c.start()
    for l in range(LAYERS):
        stored(l).wait()
    for c in sides:
        c.wait()


def gather(flags, incoming, left, right, low, high):
    vmem = pl.BlockSpec(memory_space=pltpu.VMEM)
    hbm = pl.BlockSpec(memory_space=pltpu.HBM)
    smem = pl.BlockSpec(memory_space=pltpu.SMEM)
    return pl.pallas_call(
        gather_kernel,
        out_shape=(
            jax.ShapeDtypeStruct((LAYERS, NX, NY), F32),
            jax.ShapeDtypeStruct((LAYERS, 2, 8, RUN), F32),
            jax.ShapeDtypeStruct((LAYERS, 2, 8, RUN), F32),
            jax.ShapeDtypeStruct((LAYERS, 8, NY), F32),
            jax.ShapeDtypeStruct((LAYERS, 8, NY), F32),
        ),
        in_specs=[smem] + [vmem] * 5,
        out_specs=(hbm,) * 3 + (vmem,) * 2,
        scratch_shapes=[
            pltpu.VMEM((LAYERS, 2, 8, RUN), F32),
            pltpu.VMEM((LAYERS, 2, 8, RUN), F32),
            pltpu.VMEM((LAYERS, NX, NY), F32),
            pltpu.VMEM((128, RUN), jnp.int32),
            pltpu.SMEM((128, RUN), jnp.int32),
            pltpu.SemaphoreType.DMA,
            pltpu.SemaphoreType.DMA((LAYERS,)),
            pltpu.SemaphoreType.DMA((2,)),
        ]
        + [pltpu.VMEM((POSITIONS + 8, RUN), F32)] * ACCS,
        compiler_params=pltpu.CompilerParams(vmem_limit_bytes=24 * 1024 * 1024),
    )(flags, incoming, left, right, low, high)


def corner_kernel(
    flag_ref, first_in, second_in, low_in, high_in, first_hbm, second_hbm, first_ref, second_ref, sem
):
    even_y = flag_ref[4] > 0
    even_x = flag_ref[5] > 0

    def send(l, h, low, high):
        first_ref[l, h] = jnp.where(even_x, high, low)
        second_ref[l, h] = jnp.where(even_x, low, high)

    lane = iota((8, RUN), 1)
    low = jnp.zeros((8, RUN), F32)
    high = jnp.zeros((8, RUN), F32)
    for l in range(LAYERS):
        for h in range(2):
            cols = slice(h * RUN, (h + 1) * RUN)
            send(l, h, low_in[l, :, cols], high_in[l, :, cols])
        for start, width in FIELDS:
            for side in range(2):
                place = 16 * l + 2 * start + side * width
                chosen = (lane >= place) & (lane < place + width)
                for half in range(2):
                    a = first_in[l, half]
                    b = second_in[l, half]
                    v = jnp.where(even_y, a, b) if side else jnp.where(even_y, b, a)
                    if half == 0:
                        low = jnp.where(chosen, pltpu.roll(v, (place - start) % RUN, 1), low)
                    else:
                        high = jnp.where(chosen, pltpu.roll(v, (place - start - 120) % RUN, 1), high)
    send(LAYERS, 0, low, high)
    sides = [
        pltpu.make_async_copy(first_ref, first_hbm, sem.at[0]),
        pltpu.make_async_copy(second_ref, second_hbm, sem.at[1]),
    ]
    for c in sides:
        c.start()
    for c in sides:
        c.wait()


def corners(flags, first, second, low, high):
    smem = pl.BlockSpec(memory_space=pltpu.SMEM)
    vmem = pl.BlockSpec(memory_space=pltpu.VMEM)
    shape = jax.ShapeDtypeStruct((LAYERS + 1, 2, 8, RUN), F32)
    return pl.pallas_call(
        corner_kernel,
        out_shape=(shape, shape),
        in_specs=[smem] + [vmem] * 4,
        out_specs=(pl.BlockSpec(memory_space=pltpu.HBM),) * 2,
        scratch_shapes=[pltpu.VMEM(shape.shape, F32)] * 2 + [pltpu.SemaphoreType.DMA((2,))],
        compiler_params=pltpu.CompilerParams(vmem_limit_bytes=4 * 1024 * 1024),
    )(flags, first, second, low, high)


def sweep_kernel(
    kind_ref, slope_ref, flag_ref, warmth_hbm, q_hbm, field_hbm, first_y, second_y, first_x, second_x,
    out_hbm,
    warm_a, warm_b, q_ext, field_ext, q_up, q_down, r_next, f_below, g_below, inv_row, sem,
):
    bodies = (warmth_hbm, q_hbm, field_hbm)
    exts = (warm_a, q_ext, field_ext)
    def arriving(k, l):
        return [
            pltpu.make_async_copy(
                bodies[k].at[l, :, pl.ds(h * RUN, RUN)],
                exts[k].at[l, h, pl.ds(BASE, NX), :],
                sem.at[k, l, h],
            )
            for h in range(2)
        ]

    def leaving(l):
        return [
            pltpu.make_async_copy(
                warm_b.at[l, h, pl.ds(BASE, NX), :],
                out_hbm.at[l, :, pl.ds(h * RUN, RUN)],
                sem.at[0, l, h],
            )
            for h in range(2)
        ]

    for l in range(LAYERS):
        for k in range(3):
            for c in arriving(k, l):
                c.start()
    has_left = flag_ref[0] > 0
    has_right = flag_ref[1] > 0
    has_low = flag_ref[2] > 0
    has_high = flag_ref[3] > 0
    even_y = flag_ref[4] > 0
    even_x = flag_ref[5] > 0
    fills = (0.0, WALL, 0.0)
    lane = iota((8, RUN), 1)
    sub = iota((8, RUN), 0)
    first_half = lane < 64

    def halo(l):
        def received(high, h, l):
            a = first_x[l, h]
            b = second_x[l, h]
            return jnp.where(even_x, a, b) if high else jnp.where(even_x, b, a)

        for k, (start, width) in enumerate(FIELDS):
            pick = (lane + 8 - start) % 8 < 4
            for half in range(2):
                a = first_y[l, half]
                b = second_y[l, half]
                v = jnp.where(has_left, jnp.where(even_y, b, a), fills[k])
                w = jnp.where(has_right, jnp.where(even_y, a, b), fills[k])
                both = jnp.where(pick, w, pltpu.roll(v, RUN - width, 1))
                for g in range(16):
                    row = BASE + 8 * (16 * half + g)
                    shift = (RUN - 8 * g - start) % RUN
                    exts[k][l, 2, row : row + 8, :] = pltpu.roll(both, shift, 1)
            for high, present, row in (
                (False, has_low, BASE - width),
                (True, has_high, BASE + NX),
            ):
                for h in range(2):
                    main = jnp.where(present, received(high, h, l), fills[k])
                    exts[k][l, h, row : row + width, :] = main[start : start + width]
                c = received(high, 0, LAYERS)
                c = pltpu.roll(c, RUN - (16 * l + 2 * start + width), 1)
                cl = jnp.where(present & has_left, c, fills[k])
                cr = jnp.where(present & has_right, c, fills[k])
                c = jnp.where(first_half, cr, cl)
                top = 0 if high else 8 - width
                exts[k][l, 2, row : row + width, :] = c[top : top + width]

    last = lane == RUN - 1
    first = lane == 0

    def up(v):
        s = [pltpu.roll(x, RUN - 1, 1) for x in v]
        return [jnp.where(last, s[(h + 1) % 3], s[h]) for h in range(3)]

    def down(v):
        s = [pltpu.roll(x, 1, 1) for x in v]
        return [jnp.where(first, s[(h + 2) % 3], s[h]) for h in range(3)]

    def rcp(x):
        return pl.reciprocal(x, approx=True)

    inverse = [1.0 / jnp.full((8, RUN), slope_ref[kind_ref[l]], F32) for l in range(LAYERS)]
    for l in range(LAYERS):
        inv_row[l] = inverse[l]
    top = BASE - 4
    stride = 33

    def at(j):
        return pl.ds(top + j, 8, stride=stride)

    def load(ref, l, j):
        return [ref[l, h, at(j), :] for h in range(3)]

    def one_sweep(src, dst, opening, blocks):
        every = range(blocks)

        def resist(l, j, t):
            inv = inv_row[l]
            q = load(q_ext, l, j)
            return [q[h] * (t[h] + inv) for h in every]

        def arrive(l):
            for k in range(3):
                for c in arriving(k, l):
                    c.wait()
            halo(l)

        if opening:
            arrive(0)
        for l in range(LAYERS):
            above = l < LAYERS - 1
            if opening and above:
                arrive(l + 1)
            inv = inv_row[l]

            def own(j, t):
                return [r_next[j, h] for h in every] if l > 0 else resist(l, j, t)

            def beside(j, t):
                tu, td = up(t), down(t)
                if opening:
                    q = load(q_ext, l, j)
                    qu, qd = up(q), down(q)
                    for h in range(3):
                        q_up[l, h, at(j), :] = qu[h]
                        q_down[l, h, at(j), :] = qd[h]
                else:
                    qu, qd = load(q_up, l, j), load(q_down, l, j)
                ru = [qu[h] * (tu[h] + inv) for h in every]
                rd = [qd[h] * (td[h] + inv) for h in every]
                return tu, td, ru, rd

            before = load(src, l, -1)
            t = load(src, l, 0)
            r = own(0, t)
            rb = resist(l, -1, before)
            gx = [rcp(rb[h] + r[h]) for h in every]
            px = [gx[h] * before[h] for h in every]
            for j in range(stride):
                tu, td, ru, rd = beside(j, t)
                tn = load(src, l, j + 1)
                rn = own(j + 1, tn)
                if above:
                    ta = load(src, l + 1, j)
                    ra = resist(l + 1, j, ta)
                for h in every:
                    gu = rcp(r[h] + ru[h])
                    gd = rcp(r[h] + rd[h])
                    g = rcp(r[h] + rn[h])
                    numer = field_ext[l, h, at(j), :] + px[h]
                    numer = (numer + g * tn[h]) + (gu * tu[h] + gd * td[h])
                    denom = (g + gx[h]) + (gu + gd)
                    gx[h] = g
                    px[h] = g * t[h]
                    if l > 0:
                        numer = numer + f_below[j, h]
                        denom = denom + g_below[j, h]
                    else:
                        denom = denom + SINK
                    if above:
                        gz = 0.5 * rcp(r[h] + ra[h])
                        numer = numer + gz * ta[h]
                        denom = denom + gz
                        r_next[j, h] = ra[h]
                        g_below[j, h] = gz
                        f_below[j, h] = gz * t[h]
                    dst[l, h, at(j), :] = numer * rcp(denom)
                t = tn
                r = rn
            if above:
                ra = resist(l + 1, stride, load(src, l + 1, stride))
                for h in every:
                    r_next[stride, h] = ra[h]
            if dst is warm_b and not opening:
                for c in leaving(l):
                    c.start()

    one_sweep(warm_a, warm_b, True, 3)
    one_sweep(warm_b, warm_a, False, 3)
    one_sweep(warm_a, warm_b, False, 2)
    for l in range(LAYERS):
        for c in leaving(l):
            c.wait()


def sweeps(kind, slope, flags, warmth, q, field, first_y, second_y, first_x, second_x):
    vmem = pl.BlockSpec(memory_space=pltpu.VMEM)
    smem = pl.BlockSpec(memory_space=pltpu.SMEM)
    hbm = pl.BlockSpec(memory_space=pltpu.HBM)
    ext = pltpu.VMEM((LAYERS, 3, ROWS, RUN), F32)
    row = pltpu.VMEM((34, 3, 8, RUN), F32)
    return pl.pallas_call(
        sweep_kernel,
        out_shape=jax.ShapeDtypeStruct((LAYERS, NX, NY), F32),
        in_specs=[smem, smem, smem, hbm, hbm, hbm, vmem, vmem, vmem, vmem],
        out_specs=hbm,
        scratch_shapes=[
            ext,
            ext,
            ext,
            ext,
            ext,
            ext,
            row,
            row,
            row,
            pltpu.VMEM((LAYERS, 8, RUN), F32),
            pltpu.SemaphoreType.DMA((3, LAYERS, 2)),
        ],
        compiler_params=pltpu.CompilerParams(vmem_limit_bytes=64 * 1024 * 1024 - 1600 * 1024),
    )(kind, slope, flags, warmth, q, field, first_y, second_y, first_x, second_x)


def swap(axis, first, second):
    n = lax.axis_size(axis)
    pairs = [(i, i ^ 1) for i in range(n)]
    others = [(i, (((i + 1) ^ 1) - 1) % n) for i in range(n)]
    return lax.ppermute(first, axis, pairs), lax.ppermute(second, axis, others)


def per_device(
    segment_wattage_table,
    segment_target_tile,
    occupied_slot_tally,
    segment_tile_position,
    stratum_substance,
    substance_transport_base,
    substance_thermal_slope,
    thermal_scaling_factor,
    starting_warmth_excess,
):
    tiles = 128
    outgoing = pack(
        occupied_slot_tally,
        segment_target_tile.reshape(-1, RUN),
        segment_tile_position.reshape(-1, RUN),
        segment_wattage_table,
    )
    incoming = lax.all_to_all(
        outgoing.reshape(tiles, 1, CHUNK * RUN), ("gx", "gy"), split_axis=0, concat_axis=0, tiled=True
    ).reshape(tiles * CHUNK, RUN)
    q, left, right, low, high = prepare(
        stratum_substance,
        substance_transport_base,
        substance_thermal_slope,
        starting_warmth_excess,
        thermal_scaling_factor,
    )
    i = lax.axis_index("gx")
    k = lax.axis_index("gy")
    flags = jnp.stack(
        [
            k > 0,
            k < lax.axis_size("gy") - 1,
            i > 0,
            i < lax.axis_size("gx") - 1,
            k % 2 == 0,
            i % 2 == 0,
        ]
    ).astype(jnp.int32)
    field, first, second, low, high = gather(flags, incoming, left, right, low, high)
    first_y, second_y = swap("gy", first, second)
    first, second = corners(flags, first_y, second_y, low, high)
    first_x, second_x = swap("gx", first, second)
    final = sweeps(
        stratum_substance,
        substance_thermal_slope,
        flags,
        starting_warmth_excess,
        q,
        field,
        first_y,
        second_y,
        first_x,
        second_x,
    )
    return field, final


def solution(mesh):
    return jax.shard_map(
        per_device,
        mesh=mesh,
        in_specs=(
            P(("gx", "gy"), None),
            P(("gx", "gy")),
            P(("gx", "gy")),
            P(("gx", "gy")),
            P(),
            P(),
            P(),
            P(None, "gx", "gy"),
            P(None, "gx", "gy"),
        ),
        out_specs=(P(None, "gx", "gy"), P(None, "gx", "gy")),
        check_vma=False,
    )
```

time: 116 us -> 108 us (0.931)
  Pallas kernels: 45.2 us -> 37.7 us
    pallas_call x1, Pallas kernels: 24.6 us -> 17 us  [sweeps(): pl.pallas_call(sweep_kernel, out_shape=jax.ShapeDtypeStruct((LAYERS, NX,...]
    unnamed x20 -> x22, local copies, waits for them, and re-layouts: 5.18 us -> 5.17 us
where the time goes in v3:
time: 108 us
  waiting for transfers between devices  45.7 us (42%)
  Pallas kernels  37.7 us (35%)
  starting transfers between devices  17.2 us (16%)
  local copies, waits for them, and re-layouts  5.28 us (5%)
  between operations  1.57 us (1%)
    all_to_all x1, waiting for transfers between devices, per_device(): lax.all_to_all(outgoing.reshape(tiles, 1, CHUNK * RUN), ('gx', 'gy'), spl...  34.4 us
    pallas_call x1, Pallas kernels, sweeps(): pl.pallas_call(sweep_kernel, out_shape=jax.ShapeDtypeStruct((LAYERS, NX,...  17 us
    all_to_all x1, starting transfers between devices, per_device(): lax.all_to_all(outgoing.reshape(tiles, 1, CHUNK * RUN), ('gx', 'gy'), spl...  12.1 us
    pallas_call x1, Pallas kernels, gather(): pl.pallas_call(gather_kernel, out_shape=(jax.ShapeDtypeStruct((LAYERS, NX...  10.9 us
    ppermute x2, waiting for transfers between devices, swap(): lax.ppermute(second, axis, others)  8.96 us
    pallas_call x1, Pallas kernels, pack(): pl.pallas_call(pack_kernel, out_shape=jax.ShapeDtypeStruct((tiles * CHUNK...  6.69 us
    unnamed x22, local copies, waits for them, and re-layouts  5.17 us
    ppermute x2, starting transfers between devices, swap(): lax.ppermute(second, axis, others)  2.77 us
  transfers between devices with their start and end apart: 5, of which 4 were waited for; matrix products, arithmetic and copies ran while one was open for 0% of the time, Pallas kernels for 2%

profile of v3, /device:TPU:0, one launch (start us, length us, event | category | flops | bytes accessed | tf_op | source)
XLA Modules:
  0.0 107.5 jit_solution(11525712200592194032)
XLA Ops:
  1.3 6.7 %shard_map.104 = f32[6272,128]{1,0:T(8,128)} custom-call(s32[1]{0:T(128)S(6)} %copy.12.tally_ref, s32[32,128]{1,0:T(8,128)} %bitcast.12, s32[32,128]{1,0:T(8,128)} %bitcast.13, f32[4096,128]{1,0:T(8,128)} %table_hbm.1), custom_call_target="tpu_custom_call" | custom-call | tf_op jit(solution)/shard_map/pallas_call | solution.py:89
  8.0 0.0 copy-start.6
  8.0 0.0 copy-start.7
  8.0 0.0 copy-start.8
  8.0 12.1 %all-to-all-start = ((f32[128,1,6272]{2,1,0:T(1,128)}), f32[128,1,6272]{2,1,0:T(1,128)S(1)}, u32[]{:S(2)}, u32[]{:S(2)}) async-start(f32[128,1,6272]{2,1,0:T(1,128)} %bitcast.11), calls=%async_computation | async-start | bytes 6422528 | tf_op jit(solution)/shard_map/all_to_all | solution.py:577
  20.2 0.1 stack.27
  20.3 0.0 copy-done.6
  20.3 0.0 copy-done.7
  20.3 0.0 copy-done.8
  20.3 0.0 copy-start
  20.3 1.6 %copy-done = f32[8,256,256]{2,1,0:T(8,128)S(1)} copy-done((f32[8,256,256]{2,1,0:T(8,128)S(1)}, f32[8,256,256]{2,1,0:T(8,128)}, u32[]{:S(2)}) %copy-start) | copy-done | bytes 2097176
  21.9 0.0 copy-start.2
  21.9 1.6 %copy-done.2 = f32[8,256,256]{2,1,0:T(8,128)S(1)} copy-done((f32[8,256,256]{2,1,0:T(8,128)S(1)}, f32[8,256,256]{2,1,0:T(8,128)}, u32[]{:S(2)}) %copy-start.2) | copy-done | bytes 2097176
  23.5 0.0 copy-start.5
  23.5 2.2 %shard_map.105 = (f32[8,256,256]{2,1,0:T(8,128)S(1)}, f32[8,2,8,128]{3,2,1,0:T(8,128)S(1)}, f32[8,2,8,128]{3,2,1,0:T(8,128)S(1)}, f32[8,8,256]{2,1,0:T(8,128)S(1)}, f32[8,8,256]{2,1,0:T(8,128)S(1)}) custom-call(s32[8]{0:T(128)S(1)} %copy-done.6, f32[4]{0:T(128)S(1)} %copy-done.8, f32[4]{0:T(128)S(1)} %copy-done.7, f32[8,256,256]{2,1,0:T(8,128)S(1)} %copy-done, ...), custom_call_target="tpu_custom_call" | custom-call | flops 8000000 | bytes 6300000 | tf_op jit(solution)/shard_map/pallas_call | solution.py:159
  25.8 0.0 copy-start.1
  25.8 1.3 %copy-done.1 = f32[8,256,256]{2,1,0:T(8,128)} copy-done((f32[8,256,256]{2,1,0:T(8,128)}, f32[8,256,256]{2,1,0:T(8,128)S(1)}, u32[]{:S(2)}) %copy-start.1) | copy-done | bytes 2097176
  27.1 34.4 %all-to-all-done = f32[128,1,6272]{2,1,0:T(1,128)S(1)} async-done(((f32[128,1,6272]{2,1,0:T(1,128)}), f32[128,1,6272]{2,1,0:T(1,128)S(1)}, u32[]{:S(2)}, u32[]{:S(2)}) %all-to-all-start) | async-done | bytes 3211296 | tf_op jit(solution)/shard_map/all_to_all | solution.py:577
  61.6 10.9 %shard_map.106 = (f32[8,256,256]{2,1,0:T(8,128)}, f32[8,2,8,128]{3,2,1,0:T(8,128)S(1)}, f32[8,2,8,128]{3,2,1,0:T(8,128)S(1)}, f32[8,8,256]{2,1,0:T(8,128)S(1)}, f32[8,8,256]{2,1,0:T(8,128)S(1)}) custom-call(s32[6]{0:T(128)S(1)} %convert_element_type.3.flag_ref, f32[6272,128]{1,0:T(8,128)S(1)} %bitcast.10, f32[8,2,8,128]{3,2,1,0:T(8,128)S(1)} %get-tuple-element.14.left_in, ...), custom_call_target="tpu_custom_call" | custom-call | tf_op jit(solution)/shard_map/pallas_call | solution.py:251
  72.5 2.2 %collective-permute-start = (f32[8,2,8,128]{3,2,1,0:T(8,128)S(1)}, f32[8,2,8,128]{3,2,1,0:T(8,128)S(1)}, u32[]{:S(2)}, u32[]{:S(2)}) collective-permute-start(f32[8,2,8,128]{3,2,1,0:T(8,128)S(1)} %get-tuple-element.20), channel_id=1, source_target_pairs={{0,1},{1,0},{2,3},{3,2},{4,5},{5,4},{6,7},{7,6},{8,9},{9,8},{10,11... | collective-permute-start | bytes 196616 | tf_op jit(solution)/shard_map/ppermute | solution.py:556
  74.7 1.3 %collective-permute-start.1 = (f32[8,2,8,128]{3,2,1,0:T(8,128)S(1)}, f32[8,2,8,128]{3,2,1,0:T(8,128)S(1)}, u32[]{:S(2)}, u32[]{:S(2)}) collective-permute-start(f32[8,2,8,128]{3,2,1,0:T(8,128)S(1)} %get-tuple-element.21), channel_id=1, source_target_pairs={{0,7},{1,2},{2,1},{3,4},{4,3},{5,6},{6,5},{7,0},{8,15},{9,10},{10,... | collective-permute-start | bytes 196616 | tf_op jit(solution)/shard_map/ppermute | solution.py:556
  76.0 2.3 %collective-permute-done.first_in.first_y = f32[8,2,8,128]{3,2,1,0:T(8,128)S(1)} collective-permute-done((f32[8,2,8,128]{3,2,1,0:T(8,128)S(1)}, f32[8,2,8,128]{3,2,1,0:T(8,128)S(1)}, u32[]{:S(2)}, u32[]{:S(2)}) %collective-permute-start) | collective-permute-done | bytes 65568 | tf_op jit(solution)/shard_map/ppermute | solution.py:556
  78.3 0.0 copy-start.3
  78.3 4.2 %collective-permute-done.1.second_in.second_y = f32[8,2,8,128]{3,2,1,0:T(8,128)S(1)} collective-permute-done((f32[8,2,8,128]{3,2,1,0:T(8,128)S(1)}, f32[8,2,8,128]{3,2,1,0:T(8,128)S(1)}, u32[]{:S(2)}, u32[]{:S(2)}) %collective-permute-start.1) | collective-permute-done | bytes 65568 | tf_op jit(solution)/shard_map/ppermute | solution.py:556
  82.6 0.0 copy-start.4
  82.6 0.0 copy-done.5
  82.6 0.9 shard_map.107
  83.5 0.1 collective-permute-start.2
  83.6 1.4 %collective-permute-start.3 = (f32[9,2,8,128]{3,2,1,0:T(8,128)S(1)}, f32[9,2,8,128]{3,2,1,0:T(8,128)S(1)}, u32[]{:S(2)}, u32[]{:S(2)}) collective-permute-start(f32[9,2,8,128]{3,2,1,0:T(8,128)S(1)} %get-tuple-element.25), channel_id=1, source_target_pairs={{0,120},{8,16},{16,8},{24,32},{32,24},{40,48},{48,40},{56,64},{64,... | collective-permute-start | bytes 221192 | tf_op jit(solution)/shard_map/ppermute | solution.py:556
  85.0 0.0 collective-permute-done.2.first_x
  85.0 0.0 copy-start.9
  85.0 4.7 %collective-permute-done.3.second_x = f32[9,2,8,128]{3,2,1,0:T(8,128)S(1)} collective-permute-done((f32[9,2,8,128]{3,2,1,0:T(8,128)S(1)}, f32[9,2,8,128]{3,2,1,0:T(8,128)S(1)}, u32[]{:S(2)}, u32[]{:S(2)}) %collective-permute-start.3) | collective-permute-done | bytes 73760 | tf_op jit(solution)/shard_map/ppermute | solution.py:556
  89.7 0.0 copy-start.10
  89.7 0.0 copy-done.3
  89.7 0.0 copy-done.4
  89.7 0.0 copy-done.9
  89.7 0.6 copy-done.10
  90.3 17.0 %shard_map.108 = f32[8,256,256]{2,1,0:T(8,128)} custom-call(s32[8]{0:T(128)} %kind_ref.3, f32[4]{0:T(128)} %slope_ref.3, s32[6]{0:T(128)} %copy-done.5, f32[8,256,256]{2,1,0:T(8,128)} %warmth_hbm.1, f32[8,256,256]{2,1,0:T(8,128)} %copy-done.1, f32[8,256,256]{2,1,0:T(8,128)} %get-tuple-element.12.field_hbm, f32[8,2,8,128]{3,2,1,0:T(8,128)} %copy-done.3, ...), custom_call_target="tpu_custom_call" | custom-call | tf_op jit(solution)/shard_map/pallas_call | solution.py:530
  (1 shorter events, 0.0 us)
Async XLA Ops:
  8.0 12.3 %copy-start.6 = (s32[8]{0:T(128)S(1)}, s32[8]{0:T(128)}, u32[]{:S(2)}) copy-start(s32[8]{0:T(128)} %kind_ref.3) | copy-start | bytes 100
  8.0 12.3 %copy-start.7 = (f32[4]{0:T(128)S(1)}, f32[4]{0:T(128)}, u32[]{:S(2)}) copy-start(f32[4]{0:T(128)} %slope_ref.3) | copy-start | bytes 52
  8.0 12.3 %copy-start.8 = (f32[4]{0:T(128)S(1)}, f32[4]{0:T(128)}, u32[]{:S(2)}) copy-start(f32[4]{0:T(128)} %base_ref.1) | copy-start | bytes 52
  8.0 53.6 %all-to-all-start = ((f32[128,1,6272]{2,1,0:T(1,128)}), f32[128,1,6272]{2,1,0:T(1,128)S(1)}, u32[]{:S(2)}, u32[]{:S(2)}) async-start(f32[128,1,6272]{2,1,0:T(1,128)} %bitcast.11), calls=%async_computation | async-start | bytes 6422528 | tf_op jit(solution)/shard_map/all_to_all | solution.py:577
  20.3 1.6 %copy-start = (f32[8,256,256]{2,1,0:T(8,128)S(1)}, f32[8,256,256]{2,1,0:T(8,128)}, u32[]{:S(2)}) copy-start(f32[8,256,256]{2,1,0:T(8,128)} %warmth_hbm.1) | copy-start | bytes 6291460
  21.9 1.6 %copy-start.2 = (f32[8,256,256]{2,1,0:T(8,128)S(1)}, f32[8,256,256]{2,1,0:T(8,128)}, u32[]{:S(2)}) copy-start(f32[8,256,256]{2,1,0:T(8,128)} %scale_ref.1) | copy-start | bytes 6291460
  23.5 59.1 %copy-start.5 = (s32[6]{0:T(128)}, s32[6]{0:T(128)S(1)}, u32[]{:S(2)}) copy-start(s32[6]{0:T(128)S(1)} %convert_element_type.3.flag_ref) | copy-start | bytes 76
  25.8 1.4 %copy-start.1 = (f32[8,256,256]{2,1,0:T(8,128)}, f32[8,256,256]{2,1,0:T(8,128)S(1)}, u32[]{:S(2)}) copy-start(f32[8,256,256]{2,1,0:T(8,128)S(1)} %get-tuple-element.19.q_hbm) | copy-start | bytes 6291460
  72.5 5.8 %collective-permute-start = (f32[8,2,8,128]{3,2,1,0:T(8,128)S(1)}, f32[8,2,8,128]{3,2,1,0:T(8,128)S(1)}, u32[]{:S(2)}, u32[]{:S(2)}) collective-permute-start(f32[8,2,8,128]{3,2,1,0:T(8,128)S(1)} %get-tuple-element.20), channel_id=1, source_target_pairs={{0,1},{1,0},{2,3},{3,2},{4,5},{5,4},{6,7},{7,6},{8,9},{9,8},{10,11... | collective-permute-start | bytes 196616 | tf_op jit(solution)/shard_map/ppermute | solution.py:556
  74.7 7.9 %collective-permute-start.1 = (f32[8,2,8,128]{3,2,1,0:T(8,128)S(1)}, f32[8,2,8,128]{3,2,1,0:T(8,128)S(1)}, u32[]{:S(2)}, u32[]{:S(2)}) collective-permute-start(f32[8,2,8,128]{3,2,1,0:T(8,128)S(1)} %get-tuple-element.21), channel_id=1, source_target_pairs={{0,7},{1,2},{2,1},{3,4},{4,3},{5,6},{6,5},{7,0},{8,15},{9,10},{10,... | collective-permute-start | bytes 196616 | tf_op jit(solution)/shard_map/ppermute | solution.py:556
  78.3 11.4 %copy-start.3 = (f32[8,2,8,128]{3,2,1,0:T(8,128)}, f32[8,2,8,128]{3,2,1,0:T(8,128)S(1)}, u32[]{:S(2)}) copy-start(f32[8,2,8,128]{3,2,1,0:T(8,128)S(1)} %collective-permute-done.first_in.first_y) | copy-start | bytes 196612
  82.6 7.2 %copy-start.4 = (f32[8,2,8,128]{3,2,1,0:T(8,128)}, f32[8,2,8,128]{3,2,1,0:T(8,128)S(1)}, u32[]{:S(2)}) copy-start(f32[8,2,8,128]{3,2,1,0:T(8,128)S(1)} %collective-permute-done.1.second_in.second_y) | copy-start | bytes 196612
  83.5 1.5 %collective-permute-start.2 = (f32[9,2,8,128]{3,2,1,0:T(8,128)S(1)}, f32[9,2,8,128]{3,2,1,0:T(8,128)S(1)}, u32[]{:S(2)}, u32[]{:S(2)}) collective-permute-start(f32[9,2,8,128]{3,2,1,0:T(8,128)S(1)} %get-tuple-element.24), channel_id=1, source_target_pairs={{0,8},{8,0},{16,24},{24,16},{32,40},{40,32},{48,56},{56,48},{64,72... | collective-permute-start | bytes 221192 | tf_op jit(solution)/shard_map/ppermute | solution.py:556
  83.6 6.1 %collective-permute-start.3 = (f32[9,2,8,128]{3,2,1,0:T(8,128)S(1)}, f32[9,2,8,128]{3,2,1,0:T(8,128)S(1)}, u32[]{:S(2)}, u32[]{:S(2)}) collective-permute-start(f32[9,2,8,128]{3,2,1,0:T(8,128)S(1)} %get-tuple-element.25), channel_id=1, source_target_pairs={{0,120},{8,16},{16,8},{24,32},{32,24},{40,48},{48,40},{56,64},{64,... | collective-permute-start | bytes 221192 | tf_op jit(solution)/shard_map/ppermute | solution.py:556
  85.0 4.7 %copy-start.9 = (f32[9,2,8,128]{3,2,1,0:T(8,128)}, f32[9,2,8,128]{3,2,1,0:T(8,128)S(1)}, u32[]{:S(2)}) copy-start(f32[9,2,8,128]{3,2,1,0:T(8,128)S(1)} %collective-permute-done.2.first_x) | copy-start | bytes 221188
  89.7 0.6 copy-start.10

commit v4 on v3

--- a/solution.py
+++ b/solution.py
@@ -192,7 +192,7 @@
             acc[pl.ds(spot_s[s, p], 1), :] += inc_ref[pl.ds(s * CHUNK + p, 1), :]
         return 0
 
-    lax.fori_loop(0, tiles, source, 0)
+    lax.fori_loop(0, tiles, source, 0, unroll=4)
     even = flag_ref[4] > 0
     lane = iota((8, RUN), 1)
     slot = lane // 8
@@ -545,7 +545,7 @@
             pltpu.VMEM((LAYERS, 8, RUN), F32),
             pltpu.SemaphoreType.DMA((3, LAYERS, 2)),
         ],
-        compiler_params=pltpu.CompilerParams(vmem_limit_bytes=64 * 1024 * 1024 - 1600 * 1024),
+        compiler_params=pltpu.CompilerParams(vmem_limit_bytes=53 * 1024 * 1024),
     )(kind, slope, flags, warmth, q, field, first_y, second_y, first_x, second_x)
 
 

time: 108 us -> 107 us (level)
  starting transfers between devices: 17.2 us -> 16.1 us
    pallas_call x1, Pallas kernels: 6.69 us -> 8.06 us  [pack(): pl.pallas_call(pack_kernel, out_shape=jax.ShapeDtypeStruct((tiles * CHUNK...]
    all_to_all x1, starting transfers between devices: 12.1 us -> 11 us  [per_device(): lax.all_to_all(outgoing.reshape(tiles, 1, CHUNK * RUN), ('gx', 'gy'), spl...]
    unnamed x22 -> x12, local copies, waits for them, and re-layouts: 5.17 us -> 4.55 us
where the time goes in v4:
time: 107 us; the launch traced here: 106 us
  waiting for transfers between devices  45.7 us (43%)
  Pallas kernels  38.4 us (36%)
  starting transfers between devices  16.1 us (15%)
  local copies, waits for them, and re-layouts  4.66 us (4%)
  between operations  1.56 us (1%)
    all_to_all x1, waiting for transfers between devices, per_device(): lax.all_to_all(outgoing.reshape(tiles, 1, CHUNK * RUN), ('gx', 'gy'), spl...  34.4 us
    pallas_call x1, Pallas kernels, sweeps(): pl.pallas_call(sweep_kernel, out_shape=jax.ShapeDtypeStruct((LAYERS, NX,...  16.6 us
    all_to_all x1, starting transfers between devices, per_device(): lax.all_to_all(outgoing.reshape(tiles, 1, CHUNK * RUN), ('gx', 'gy'), spl...  11 us
    pallas_call x1, Pallas kernels, gather(): pl.pallas_call(gather_kernel, out_shape=(jax.ShapeDtypeStruct((LAYERS, NX...  10.6 us
    ppermute x2, waiting for transfers between devices, swap(): lax.ppermute(second, axis, others)  8.96 us
    pallas_call x1, Pallas kernels, pack(): pl.pallas_call(pack_kernel, out_shape=jax.ShapeDtypeStruct((tiles * CHUNK...  8.06 us
    unnamed x12, local copies, waits for them, and re-layouts  4.55 us
    ppermute x2, starting transfers between devices, swap(): lax.ppermute(second, axis, others)  2.76 us
  transfers between devices with their start and end apart: 5, of which 4 were waited for; matrix products, arithmetic and copies ran while one was open for 0% of the time, Pallas kernels for 2%

profile of v4, /device:TPU:0, one launch (start us, length us, event | category | flops | bytes accessed | tf_op | source)
XLA Modules:
  0.0 106.4 jit_solution(5321347310114953699)
XLA Ops:
  1.3 8.1 %shard_map.104 = f32[6272,128]{1,0:T(8,128)} custom-call(s32[1]{0:T(128)S(6)} %copy.12.tally_ref, s32[32,128]{1,0:T(8,128)} %bitcast.12, s32[32,128]{1,0:T(8,128)} %bitcast.13, f32[4096,128]{1,0:T(8,128)} %table_hbm.1), custom_call_target="tpu_custom_call" | custom-call | tf_op jit(solution)/shard_map/pallas_call | solution.py:89
  9.3 0.0 copy-start.3
  9.4 0.0 copy-start.4
  9.4 0.0 copy-start.5
  9.4 11.0 %all-to-all-start = ((f32[128,1,6272]{2,1,0:T(1,128)}), f32[128,1,6272]{2,1,0:T(1,128)S(1)}, u32[]{:S(2)}, u32[]{:S(2)}) async-start(f32[128,1,6272]{2,1,0:T(1,128)} %bitcast.11), calls=%async_computation | async-start | bytes 6422528 | tf_op jit(solution)/shard_map/all_to_all | solution.py:577
  20.5 0.1 stack.27
  20.6 0.0 copy-done.3
  20.6 0.0 copy-done.4
  20.6 0.0 copy-done.5
  20.6 0.0 copy-start
  20.6 1.6 %copy-done = f32[8,256,256]{2,1,0:T(8,128)S(1)} copy-done((f32[8,256,256]{2,1,0:T(8,128)S(1)}, f32[8,256,256]{2,1,0:T(8,128)}, u32[]{:S(2)}) %copy-start) | copy-done | bytes 2097176
  22.2 0.0 copy-start.2
  22.2 1.6 %copy-done.2 = f32[8,256,256]{2,1,0:T(8,128)S(1)} copy-done((f32[8,256,256]{2,1,0:T(8,128)S(1)}, f32[8,256,256]{2,1,0:T(8,128)}, u32[]{:S(2)}) %copy-start.2) | copy-done | bytes 2097176
  23.8 2.2 %shard_map.105 = (f32[8,256,256]{2,1,0:T(8,128)S(1)}, f32[8,2,8,128]{3,2,1,0:T(8,128)S(1)}, f32[8,2,8,128]{3,2,1,0:T(8,128)S(1)}, f32[8,8,256]{2,1,0:T(8,128)S(1)}, f32[8,8,256]{2,1,0:T(8,128)S(1)}) custom-call(s32[8]{0:T(128)S(1)} %copy-done.3, f32[4]{0:T(128)S(1)} %copy-done.5, f32[4]{0:T(128)S(1)} %copy-done.4, f32[8,256,256]{2,1,0:T(8,128)S(1)} %copy-done, ...), custom_call_target="tpu_custom_call" | custom-call | flops 8000000 | bytes 6300000 | tf_op jit(solution)/shard_map/pallas_call | solution.py:159
  26.0 0.0 copy-start.1
  26.0 1.4 %copy-done.1 = f32[8,256,256]{2,1,0:T(8,128)} copy-done((f32[8,256,256]{2,1,0:T(8,128)}, f32[8,256,256]{2,1,0:T(8,128)S(1)}, u32[]{:S(2)}) %copy-start.1) | copy-done | bytes 2097176
  27.4 34.4 %all-to-all-done = f32[128,1,6272]{2,1,0:T(1,128)S(1)} async-done(((f32[128,1,6272]{2,1,0:T(1,128)}), f32[128,1,6272]{2,1,0:T(1,128)S(1)}, u32[]{:S(2)}, u32[]{:S(2)}) %all-to-all-start) | async-done | bytes 3211296 | tf_op jit(solution)/shard_map/all_to_all | solution.py:577
  61.8 10.6 %shard_map.106 = (f32[8,256,256]{2,1,0:T(8,128)}, f32[8,2,8,128]{3,2,1,0:T(8,128)S(1)}, f32[8,2,8,128]{3,2,1,0:T(8,128)S(1)}, f32[8,8,256]{2,1,0:T(8,128)S(1)}, f32[8,8,256]{2,1,0:T(8,128)S(1)}) custom-call(s32[6]{0:T(128)S(1)} %convert_element_type.3.flag_ref, f32[6272,128]{1,0:T(8,128)S(1)} %bitcast.10, f32[8,2,8,128]{3,2,1,0:T(8,128)S(1)} %get-tuple-element.14.left_in, ...), custom_call_target="tpu_custom_call" | custom-call | tf_op jit(solution)/shard_map/pallas_call | solution.py:251
  72.4 2.2 %collective-permute-start = (f32[8,2,8,128]{3,2,1,0:T(8,128)S(1)}, f32[8,2,8,128]{3,2,1,0:T(8,128)S(1)}, u32[]{:S(2)}, u32[]{:S(2)}) collective-permute-start(f32[8,2,8,128]{3,2,1,0:T(8,128)S(1)} %get-tuple-element.20), channel_id=1, source_target_pairs={{0,1},{1,0},{2,3},{3,2},{4,5},{5,4},{6,7},{7,6},{8,9},{9,8},{10,11... | collective-permute-start | bytes 196616 | tf_op jit(solution)/shard_map/ppermute | solution.py:556
  74.7 1.3 %collective-permute-start.1 = (f32[8,2,8,128]{3,2,1,0:T(8,128)S(1)}, f32[8,2,8,128]{3,2,1,0:T(8,128)S(1)}, u32[]{:S(2)}, u32[]{:S(2)}) collective-permute-start(f32[8,2,8,128]{3,2,1,0:T(8,128)S(1)} %get-tuple-element.21), channel_id=1, source_target_pairs={{0,7},{1,2},{2,1},{3,4},{4,3},{5,6},{6,5},{7,0},{8,15},{9,10},{10,... | collective-permute-start | bytes 196616 | tf_op jit(solution)/shard_map/ppermute | solution.py:556
  76.0 2.3 %collective-permute-done.first_in.first_y = f32[8,2,8,128]{3,2,1,0:T(8,128)S(1)} collective-permute-done((f32[8,2,8,128]{3,2,1,0:T(8,128)S(1)}, f32[8,2,8,128]{3,2,1,0:T(8,128)S(1)}, u32[]{:S(2)}, u32[]{:S(2)}) %collective-permute-start) | collective-permute-done | bytes 65568 | tf_op jit(solution)/shard_map/ppermute | solution.py:556
  78.3 4.2 %collective-permute-done.1.second_in.second_y = f32[8,2,8,128]{3,2,1,0:T(8,128)S(1)} collective-permute-done((f32[8,2,8,128]{3,2,1,0:T(8,128)S(1)}, f32[8,2,8,128]{3,2,1,0:T(8,128)S(1)}, u32[]{:S(2)}, u32[]{:S(2)}) %collective-permute-start.1) | collective-permute-done | bytes 65568 | tf_op jit(solution)/shard_map/ppermute | solution.py:556
  82.5 0.9 shard_map.107
  83.5 0.1 collective-permute-start.2
  83.5 1.4 %collective-permute-start.3 = (f32[9,2,8,128]{3,2,1,0:T(8,128)S(1)}, f32[9,2,8,128]{3,2,1,0:T(8,128)S(1)}, u32[]{:S(2)}, u32[]{:S(2)}) collective-permute-start(f32[9,2,8,128]{3,2,1,0:T(8,128)S(1)} %get-tuple-element.25), channel_id=1, source_target_pairs={{0,120},{8,16},{16,8},{24,32},{32,24},{40,48},{48,40},{56,64},{64,... | collective-permute-start | bytes 221192 | tf_op jit(solution)/shard_map/ppermute | solution.py:556
  85.0 0.0 collective-permute-done.2.first_x
  85.0 4.7 %collective-permute-done.3.second_x = f32[9,2,8,128]{3,2,1,0:T(8,128)S(1)} collective-permute-done((f32[9,2,8,128]{3,2,1,0:T(8,128)S(1)}, f32[9,2,8,128]{3,2,1,0:T(8,128)S(1)}, u32[]{:S(2)}, u32[]{:S(2)}) %collective-permute-start.3) | collective-permute-done | bytes 73760 | tf_op jit(solution)/shard_map/ppermute | solution.py:556
  89.7 16.6 %shard_map.108 = f32[8,256,256]{2,1,0:T(8,128)} custom-call(s32[8]{0:T(128)S(1)} %copy-done.3, f32[4]{0:T(128)S(1)} %copy-done.4, s32[6]{0:T(128)S(1)} %convert_element_type.3.flag_ref, f32[8,256,256]{2,1,0:T(8,128)} %warmth_hbm.1, f32[8,256,256]{2,1,0:T(8,128)} %copy-done.1, f32[8,256,256]{2,1,0:T(8,128)} %get-tuple-element.12.field_hbm, ...), custom_call_target="tpu_custom_call" | custom-call | tf_op jit(solution)/shard_map/pallas_call | solution.py:530
  (1 shorter events, 0.0 us)
Async XLA Ops:
  9.3 11.2 %copy-start.3 = (s32[8]{0:T(128)S(1)}, s32[8]{0:T(128)}, u32[]{:S(2)}) copy-start(s32[8]{0:T(128)} %kind_ref.3) | copy-start | bytes 100
  9.4 11.2 %copy-start.4 = (f32[4]{0:T(128)S(1)}, f32[4]{0:T(128)}, u32[]{:S(2)}) copy-start(f32[4]{0:T(128)} %slope_ref.3) | copy-start | bytes 52
  9.4 11.2 %copy-start.5 = (f32[4]{0:T(128)S(1)}, f32[4]{0:T(128)}, u32[]{:S(2)}) copy-start(f32[4]{0:T(128)} %base_ref.1) | copy-start | bytes 52
  9.4 52.4 %all-to-all-start = ((f32[128,1,6272]{2,1,0:T(1,128)}), f32[128,1,6272]{2,1,0:T(1,128)S(1)}, u32[]{:S(2)}, u32[]{:S(2)}) async-start(f32[128,1,6272]{2,1,0:T(1,128)} %bitcast.11), calls=%async_computation | async-start | bytes 6422528 | tf_op jit(solution)/shard_map/all_to_all | solution.py:577
  20.6 1.6 %copy-start = (f32[8,256,256]{2,1,0:T(8,128)S(1)}, f32[8,256,256]{2,1,0:T(8,128)}, u32[]{:S(2)}) copy-start(f32[8,256,256]{2,1,0:T(8,128)} %warmth_hbm.1) | copy-start | bytes 6291460
  22.2 1.6 %copy-start.2 = (f32[8,256,256]{2,1,0:T(8,128)S(1)}, f32[8,256,256]{2,1,0:T(8,128)}, u32[]{:S(2)}) copy-start(f32[8,256,256]{2,1,0:T(8,128)} %scale_ref.1) | copy-start | bytes 6291460
  26.0 1.4 %copy-start.1 = (f32[8,256,256]{2,1,0:T(8,128)}, f32[8,256,256]{2,1,0:T(8,128)S(1)}, u32[]{:S(2)}) copy-start(f32[8,256,256]{2,1,0:T(8,128)S(1)} %get-tuple-element.19.q_hbm) | copy-start | bytes 6291460
  72.4 5.8 %collective-permute-start = (f32[8,2,8,128]{3,2,1,0:T(8,128)S(1)}, f32[8,2,8,128]{3,2,1,0:T(8,128)S(1)}, u32[]{:S(2)}, u32[]{:S(2)}) collective-permute-start(f32[8,2,8,128]{3,2,1,0:T(8,128)S(1)} %get-tuple-element.20), channel_id=1, source_target_pairs={{0,1},{1,0},{2,3},{3,2},{4,5},{5,4},{6,7},{7,6},{8,9},{9,8},{10,11... | collective-permute-start | bytes 196616 | tf_op jit(solution)/shard_map/ppermute | solution.py:556
  74.7 7.9 %collective-permute-start.1 = (f32[8,2,8,128]{3,2,1,0:T(8,128)S(1)}, f32[8,2,8,128]{3,2,1,0:T(8,128)S(1)}, u32[]{:S(2)}, u32[]{:S(2)}) collective-permute-start(f32[8,2,8,128]{3,2,1,0:T(8,128)S(1)} %get-tuple-element.21), channel_id=1, source_target_pairs={{0,7},{1,2},{2,1},{3,4},{4,3},{5,6},{6,5},{7,0},{8,15},{9,10},{10,... | collective-permute-start | bytes 196616 | tf_op jit(solution)/shard_map/ppermute | solution.py:556
  83.5 1.5 %collective-permute-start.2 = (f32[9,2,8,128]{3,2,1,0:T(8,128)S(1)}, f32[9,2,8,128]{3,2,1,0:T(8,128)S(1)}, u32[]{:S(2)}, u32[]{:S(2)}) collective-permute-start(f32[9,2,8,128]{3,2,1,0:T(8,128)S(1)} %get-tuple-element.24), channel_id=1, source_target_pairs={{0,8},{8,0},{16,24},{24,16},{32,40},{40,32},{48,56},{56,48},{64,72... | collective-permute-start | bytes 221192 | tf_op jit(solution)/shard_map/ppermute | solution.py:556
  83.5 6.1 %collective-permute-start.3 = (f32[9,2,8,128]{3,2,1,0:T(8,128)S(1)}, f32[9,2,8,128]{3,2,1,0:T(8,128)S(1)}, u32[]{:S(2)}, u32[]{:S(2)}) collective-permute-start(f32[9,2,8,128]{3,2,1,0:T(8,128)S(1)} %get-tuple-element.25), channel_id=1, source_target_pairs={{0,120},{8,16},{16,8},{24,32},{32,24},{40,48},{48,40},{56,64},{64,... | collective-permute-start | bytes 221192 | tf_op jit(solution)/shard_map/ppermute | solution.py:556

commit v5 on v4

--- a/solution.py
+++ b/solution.py
@@ -30,7 +30,7 @@
 
 
 def pack_kernel(
-    tally_ref, target_ref, place_ref, table_hbm, out_ref, table_ref, dest_v, dest_s, sem, table_sem
+    tally_ref, target_ref, place_ref, table_hbm, out_ref, table_ref, dest_v, dest_s, dest_sem, table_sem
 ):
     load = pltpu.make_async_copy(table_hbm, table_ref, table_sem)
     load.start()
@@ -66,11 +66,17 @@
         return seen + run[:, RUN:], placed
 
     zero = jnp.zeros((tiles, RUN), F32)
-    seen, placed = lax.fori_loop(0, 32, rank_group, (zero, zero), unroll=32)
-    placed = placed + 64.0 * pltpu.roll(placed, 64, 1)
-    copy = pltpu.make_async_copy(dest_v, dest_s, sem)
-    copy.start()
-    copy.wait()
+    carry = (zero, zero)
+    halves = [
+        pltpu.make_async_copy(
+            dest_v.at[pl.ds(16 * i, 16), :], dest_s.at[pl.ds(16 * i, 16), :], dest_sem.at[i]
+        )
+        for i in range(2)
+    ]
+    for i in range(2):
+        carry = lax.fori_loop(16 * i, 16 * i + 16, rank_group, carry, unroll=16)
+        halves[i].start()
+    placed = carry[1] + 64.0 * pltpu.roll(carry[1], 64, 1)
 
     load.wait()
 
@@ -79,9 +85,12 @@
             out_ref[pl.ds(dest_s[g, k], 1), :] = table_ref[pl.ds(g * RUN + k, 1), :]
         return 0
 
-    lax.fori_loop(0, (tally + RUN - 1) // RUN, move, 0)
-    for t in range(tiles):
-        out_ref[t * CHUNK + CAP : t * CHUNK + CAP + 1, :] = placed[t : t + 1, :]
+    groups = (tally + RUN - 1) // RUN
+    halves[0].wait()
+    lax.fori_loop(0, jnp.minimum(groups, 16), move, 0)
+    halves[1].wait()
+    lax.fori_loop(16, jnp.maximum(groups, 16), move, 0)
+    out_ref[pl.ds(CAP, tiles, stride=CHUNK), :] = placed
 
 
 def pack(tally, target, place, table):
@@ -100,7 +109,7 @@
             pltpu.VMEM((32 * RUN, RUN), F32),
             pltpu.VMEM((32, RUN), jnp.int32),
             pltpu.SMEM((32, RUN), jnp.int32),
-            pltpu.SemaphoreType.DMA,
+            pltpu.SemaphoreType.DMA((2,)),
             pltpu.SemaphoreType.DMA,
         ],
         compiler_params=pltpu.CompilerParams(vmem_limit_bytes=VMEM_LIMIT),
@@ -168,13 +177,12 @@
 
 def gather_kernel(
     flag_ref, inc_ref, left_in, right_in, low_in, high_in,
-    field_hbm, first_hbm, second_hbm, low_ref, high_ref,
-    first_ref, second_ref, field_ref, spot_v, spot_s, spot_sem, field_sem, side_sem, *accs,
+    field_hbm, first_ref, second_ref, low_ref, high_ref,
+    field_ref, spot_v, spot_s, spot_sem, field_sem, *accs,
 ):
     tiles = 128
-    for t in range(tiles):
-        row = inc_ref[t * CHUNK + CAP : t * CHUNK + CAP + 1, :]
-        spot_v[t : t + 1, :] = jnp.where(row > 0.5, row.astype(jnp.int32) - 1, POSITIONS)
+    marks = inc_ref[pl.ds(CAP, tiles, stride=CHUNK), :]
+    spot_v[...] = jnp.where(marks > 0.5, marks.astype(jnp.int32) - 1, POSITIONS)
     copy = pltpu.make_async_copy(spot_v, spot_s, spot_sem)
     copy.start()
 
@@ -232,16 +240,8 @@
         return 0
 
     lax.fori_loop(0, LAYERS, layer, 0)
-    sides = [
-        pltpu.make_async_copy(first_ref, first_hbm, side_sem.at[0]),
-        pltpu.make_async_copy(second_ref, second_hbm, side_sem.at[1]),
-    ]
-    for c in sides:
-        c.start()
     for l in range(LAYERS):
         stored(l).wait()
-    for c in sides:
-        c.wait()
 
 
 def gather(flags, incoming, left, right, low, high):
@@ -258,25 +258,20 @@
             jax.ShapeDtypeStruct((LAYERS, 8, NY), F32),
         ),
         in_specs=[smem] + [vmem] * 5,
-        out_specs=(hbm,) * 3 + (vmem,) * 2,
+        out_specs=(hbm,) + (vmem,) * 4,
         scratch_shapes=[
-            pltpu.VMEM((LAYERS, 2, 8, RUN), F32),
-            pltpu.VMEM((LAYERS, 2, 8, RUN), F32),
             pltpu.VMEM((LAYERS, NX, NY), F32),
             pltpu.VMEM((128, RUN), jnp.int32),
             pltpu.SMEM((128, RUN), jnp.int32),
             pltpu.SemaphoreType.DMA,
             pltpu.SemaphoreType.DMA((LAYERS,)),
-            pltpu.SemaphoreType.DMA((2,)),
         ]
         + [pltpu.VMEM((POSITIONS + 8, RUN), F32)] * ACCS,
         compiler_params=pltpu.CompilerParams(vmem_limit_bytes=24 * 1024 * 1024),
     )(flags, incoming, left, right, low, high)
 
 
-def corner_kernel(
-    flag_ref, first_in, second_in, low_in, high_in, first_hbm, second_hbm, first_ref, second_ref, sem
-):
+def corner_kernel(flag_ref, first_in, second_in, low_in, high_in, first_ref, second_ref):
     even_y = flag_ref[4] > 0
     even_x = flag_ref[5] > 0
 
@@ -304,14 +299,9 @@
                     else:
                         high = jnp.where(chosen, pltpu.roll(v, (place - start - 120) % RUN, 1), high)
     send(LAYERS, 0, low, high)
-    sides = [
-        pltpu.make_async_copy(first_ref, first_hbm, sem.at[0]),
-        pltpu.make_async_copy(second_ref, second_hbm, sem.at[1]),
-    ]
-    for c in sides:
-        c.start()
-    for c in sides:
-        c.wait()
+    blank = jnp.zeros((8, RUN), F32)
+    first_ref[LAYERS, 1] = blank
+    second_ref[LAYERS, 1] = blank
 
 
 def corners(flags, first, second, low, high):
@@ -322,8 +312,7 @@
         corner_kernel,
         out_shape=(shape, shape),
         in_specs=[smem] + [vmem] * 4,
-        out_specs=(pl.BlockSpec(memory_space=pltpu.HBM),) * 2,
-        scratch_shapes=[pltpu.VMEM(shape.shape, F32)] * 2 + [pltpu.SemaphoreType.DMA((2,))],
+        out_specs=(vmem,) * 2,
         compiler_params=pltpu.CompilerParams(vmem_limit_bytes=4 * 1024 * 1024),
     )(flags, first, second, low, high)
 

time: 107 us -> 106 us (level)
  Pallas kernels: 38.4 us -> 37.3 us
where the time goes in v5:
time: 106 us
  waiting for transfers between devices  45.7 us (43%)
  Pallas kernels  37.3 us (35%)
  starting transfers between devices  16.4 us (15%)
  local copies, waits for them, and re-layouts  4.66 us (4%)
  between operations  1.56 us (1%)
    all_to_all x1, waiting for transfers between devices, per_device(): lax.all_to_all(outgoing.reshape(tiles, 1, CHUNK * RUN), ('gx', 'gy'), spl...  34.4 us
    pallas_call x1, Pallas kernels, sweeps(): pl.pallas_call(sweep_kernel, out_shape=jax.ShapeDtypeStruct((LAYERS, NX,...  16.6 us
    all_to_all x1, starting transfers between devices, per_device(): lax.all_to_all(outgoing.reshape(tiles, 1, CHUNK * RUN), ('gx', 'gy'), spl...  11.3 us
    pallas_call x1, Pallas kernels, gather(): pl.pallas_call(gather_kernel, out_shape=(jax.ShapeDtypeStruct((LAYERS, NX...  10.5 us
    ppermute x2, waiting for transfers between devices, swap(): lax.ppermute(second, axis, others)  8.97 us
    pallas_call x1, Pallas kernels, pack(): pl.pallas_call(pack_kernel, out_shape=jax.ShapeDtypeStruct((tiles * CHUNK...  7.3 us
    unnamed x12, local copies, waits for them, and re-layouts  4.55 us
    ppermute x2, starting transfers between devices, swap(): lax.ppermute(second, axis, others)  2.77 us
  transfers between devices with their start and end apart: 5, of which 4 were waited for; matrix products, arithmetic and copies ran while one was open for 0% of the time, Pallas kernels for 2%

profile of v5, /device:TPU:0, one launch (start us, length us, event | category | flops | bytes accessed | tf_op | source)
XLA Modules:
  0.0 105.5 jit_solution(13319557988576389464)
XLA Ops:
  1.3 7.3 %shard_map.104 = f32[6272,128]{1,0:T(8,128)} custom-call(s32[1]{0:T(128)S(6)} %copy.12.tally_ref, s32[32,128]{1,0:T(8,128)} %bitcast.12, s32[32,128]{1,0:T(8,128)} %bitcast.13, f32[4096,128]{1,0:T(8,128)} %table_hbm.1), custom_call_target="tpu_custom_call" | custom-call | tf_op jit(solution)/shard_map/pallas_call | solution.py:98
  8.6 0.0 copy-start.3
  8.6 0.0 copy-start.4
  8.6 0.0 copy-start.5
  8.6 11.3 %all-to-all-start = ((f32[128,1,6272]{2,1,0:T(1,128)}), f32[128,1,6272]{2,1,0:T(1,128)S(1)}, u32[]{:S(2)}, u32[]{:S(2)}) async-start(f32[128,1,6272]{2,1,0:T(1,128)} %bitcast.11), calls=%async_computation | async-start | bytes 6422528 | tf_op jit(solution)/shard_map/all_to_all | solution.py:566
  19.9 0.1 stack.27
  20.1 0.0 copy-done.3
  20.1 0.0 copy-done.4
  20.1 0.0 copy-done.5
  20.1 0.0 copy-start
  20.1 1.6 %copy-done = f32[8,256,256]{2,1,0:T(8,128)S(1)} copy-done((f32[8,256,256]{2,1,0:T(8,128)S(1)}, f32[8,256,256]{2,1,0:T(8,128)}, u32[]{:S(2)}) %copy-start) | copy-done | bytes 2097176
  21.7 0.0 copy-start.2
  21.7 1.6 %copy-done.2 = f32[8,256,256]{2,1,0:T(8,128)S(1)} copy-done((f32[8,256,256]{2,1,0:T(8,128)S(1)}, f32[8,256,256]{2,1,0:T(8,128)}, u32[]{:S(2)}) %copy-start.2) | copy-done | bytes 2097176
  23.3 2.2 %shard_map.105 = (f32[8,256,256]{2,1,0:T(8,128)S(1)}, f32[8,2,8,128]{3,2,1,0:T(8,128)S(1)}, f32[8,2,8,128]{3,2,1,0:T(8,128)S(1)}, f32[8,8,256]{2,1,0:T(8,128)S(1)}, f32[8,8,256]{2,1,0:T(8,128)S(1)}) custom-call(s32[8]{0:T(128)S(1)} %copy-done.3, f32[4]{0:T(128)S(1)} %copy-done.5, f32[4]{0:T(128)S(1)} %copy-done.4, f32[8,256,256]{2,1,0:T(8,128)S(1)} %copy-done, ...), custom_call_target="tpu_custom_call" | custom-call | flops 8000000 | bytes 6300000 | tf_op jit(solution)/shard_map/pallas_call | solution.py:168
  25.5 0.0 copy-start.1
  25.5 1.4 %copy-done.1 = f32[8,256,256]{2,1,0:T(8,128)} copy-done((f32[8,256,256]{2,1,0:T(8,128)}, f32[8,256,256]{2,1,0:T(8,128)S(1)}, u32[]{:S(2)}) %copy-start.1) | copy-done | bytes 2097176
  26.9 34.4 %all-to-all-done = f32[128,1,6272]{2,1,0:T(1,128)S(1)} async-done(((f32[128,1,6272]{2,1,0:T(1,128)}), f32[128,1,6272]{2,1,0:T(1,128)S(1)}, u32[]{:S(2)}, u32[]{:S(2)}) %all-to-all-start) | async-done | bytes 3211296 | tf_op jit(solution)/shard_map/all_to_all | solution.py:566
  61.3 10.5 %shard_map.106 = (f32[8,256,256]{2,1,0:T(8,128)}, f32[8,2,8,128]{3,2,1,0:T(8,128)S(1)}, f32[8,2,8,128]{3,2,1,0:T(8,128)S(1)}, f32[8,8,256]{2,1,0:T(8,128)S(1)}, f32[8,8,256]{2,1,0:T(8,128)S(1)}) custom-call(s32[6]{0:T(128)S(1)} %convert_element_type.3.flag_ref, f32[6272,128]{1,0:T(8,128)S(1)} %bitcast.10, f32[8,2,8,128]{3,2,1,0:T(8,128)S(1)} %get-tuple-element.14.left_in, ...), custom_call_target="tpu_custom_call" | custom-call | tf_op jit(solution)/shard_map/pallas_call | solution.py:251
  71.8 2.2 %collective-permute-start = (f32[8,2,8,128]{3,2,1,0:T(8,128)S(1)}, f32[8,2,8,128]{3,2,1,0:T(8,128)S(1)}, u32[]{:S(2)}, u32[]{:S(2)}) collective-permute-start(f32[8,2,8,128]{3,2,1,0:T(8,128)S(1)} %get-tuple-element.20), channel_id=1, source_target_pairs={{0,1},{1,0},{2,3},{3,2},{4,5},{5,4},{6,7},{7,6},{8,9},{9,8},{10,11... | collective-permute-start | bytes 196616 | tf_op jit(solution)/shard_map/ppermute | solution.py:545
  74.0 1.4 %collective-permute-start.1 = (f32[8,2,8,128]{3,2,1,0:T(8,128)S(1)}, f32[8,2,8,128]{3,2,1,0:T(8,128)S(1)}, u32[]{:S(2)}, u32[]{:S(2)}) collective-permute-start(f32[8,2,8,128]{3,2,1,0:T(8,128)S(1)} %get-tuple-element.21), channel_id=1, source_target_pairs={{0,7},{1,2},{2,1},{3,4},{4,3},{5,6},{6,5},{7,0},{8,15},{9,10},{10,... | collective-permute-start | bytes 196616 | tf_op jit(solution)/shard_map/ppermute | solution.py:545
  75.3 2.3 %collective-permute-done.first_in.first_y = f32[8,2,8,128]{3,2,1,0:T(8,128)S(1)} collective-permute-done((f32[8,2,8,128]{3,2,1,0:T(8,128)S(1)}, f32[8,2,8,128]{3,2,1,0:T(8,128)S(1)}, u32[]{:S(2)}, u32[]{:S(2)}) %collective-permute-start) | collective-permute-done | bytes 65568 | tf_op jit(solution)/shard_map/ppermute | solution.py:545
  77.6 4.2 %collective-permute-done.1.second_in.second_y = f32[8,2,8,128]{3,2,1,0:T(8,128)S(1)} collective-permute-done((f32[8,2,8,128]{3,2,1,0:T(8,128)S(1)}, f32[8,2,8,128]{3,2,1,0:T(8,128)S(1)}, u32[]{:S(2)}, u32[]{:S(2)}) %collective-permute-start.1) | collective-permute-done | bytes 65568 | tf_op jit(solution)/shard_map/ppermute | solution.py:545
  81.9 0.7 shard_map.107
  82.6 0.1 collective-permute-start.2
  82.7 1.4 %collective-permute-start.3 = (f32[9,2,8,128]{3,2,1,0:T(8,128)S(1)}, f32[9,2,8,128]{3,2,1,0:T(8,128)S(1)}, u32[]{:S(2)}, u32[]{:S(2)}) collective-permute-start(f32[9,2,8,128]{3,2,1,0:T(8,128)S(1)} %get-tuple-element.25), channel_id=1, source_target_pairs={{0,120},{8,16},{16,8},{24,32},{32,24},{40,48},{48,40},{56,64},{64,... | collective-permute-start | bytes 221192 | tf_op jit(solution)/shard_map/ppermute | solution.py:545
  84.1 0.0 collective-permute-done.2.first_x
  84.1 4.7 %collective-permute-done.3.second_x = f32[9,2,8,128]{3,2,1,0:T(8,128)S(1)} collective-permute-done((f32[9,2,8,128]{3,2,1,0:T(8,128)S(1)}, f32[9,2,8,128]{3,2,1,0:T(8,128)S(1)}, u32[]{:S(2)}, u32[]{:S(2)}) %collective-permute-start.3) | collective-permute-done | bytes 73760 | tf_op jit(solution)/shard_map/ppermute | solution.py:545
  88.8 16.6 %shard_map.108 = f32[8,256,256]{2,1,0:T(8,128)} custom-call(s32[8]{0:T(128)S(1)} %copy-done.3, f32[4]{0:T(128)S(1)} %copy-done.4, s32[6]{0:T(128)S(1)} %convert_element_type.3.flag_ref, f32[8,256,256]{2,1,0:T(8,128)} %warmth_hbm.1, f32[8,256,256]{2,1,0:T(8,128)} %copy-done.1, f32[8,256,256]{2,1,0:T(8,128)} %get-tuple-element.12.field_hbm, ...), custom_call_target="tpu_custom_call" | custom-call | tf_op jit(solution)/shard_map/pallas_call | solution.py:519
  (1 shorter events, 0.0 us)
Async XLA Ops:
  8.6 11.5 %copy-start.3 = (s32[8]{0:T(128)S(1)}, s32[8]{0:T(128)}, u32[]{:S(2)}) copy-start(s32[8]{0:T(128)} %kind_ref.3) | copy-start | bytes 100
  8.6 11.5 %copy-start.4 = (f32[4]{0:T(128)S(1)}, f32[4]{0:T(128)}, u32[]{:S(2)}) copy-start(f32[4]{0:T(128)} %slope_ref.3) | copy-start | bytes 52
  8.6 11.5 %copy-start.5 = (f32[4]{0:T(128)S(1)}, f32[4]{0:T(128)}, u32[]{:S(2)}) copy-start(f32[4]{0:T(128)} %base_ref.1) | copy-start | bytes 52
  8.6 52.7 %all-to-all-start = ((f32[128,1,6272]{2,1,0:T(1,128)}), f32[128,1,6272]{2,1,0:T(1,128)S(1)}, u32[]{:S(2)}, u32[]{:S(2)}) async-start(f32[128,1,6272]{2,1,0:T(1,128)} %bitcast.11), calls=%async_computation | async-start | bytes 6422528 | tf_op jit(solution)/shard_map/all_to_all | solution.py:566
  20.1 1.6 %copy-start = (f32[8,256,256]{2,1,0:T(8,128)S(1)}, f32[8,256,256]{2,1,0:T(8,128)}, u32[]{:S(2)}) copy-start(f32[8,256,256]{2,1,0:T(8,128)} %warmth_hbm.1) | copy-start | bytes 6291460
  21.7 1.6 %copy-start.2 = (f32[8,256,256]{2,1,0:T(8,128)S(1)}, f32[8,256,256]{2,1,0:T(8,128)}, u32[]{:S(2)}) copy-start(f32[8,256,256]{2,1,0:T(8,128)} %scale_ref.1) | copy-start | bytes 6291460
  25.5 1.4 %copy-start.1 = (f32[8,256,256]{2,1,0:T(8,128)}, f32[8,256,256]{2,1,0:T(8,128)S(1)}, u32[]{:S(2)}) copy-start(f32[8,256,256]{2,1,0:T(8,128)S(1)} %get-tuple-element.19.q_hbm) | copy-start | bytes 6291460
  71.8 5.8 %collective-permute-start = (f32[8,2,8,128]{3,2,1,0:T(8,128)S(1)}, f32[8,2,8,128]{3,2,1,0:T(8,128)S(1)}, u32[]{:S(2)}, u32[]{:S(2)}) collective-permute-start(f32[8,2,8,128]{3,2,1,0:T(8,128)S(1)} %get-tuple-element.20), channel_id=1, source_target_pairs={{0,1},{1,0},{2,3},{3,2},{4,5},{5,4},{6,7},{7,6},{8,9},{9,8},{10,11... | collective-permute-start | bytes 196616 | tf_op jit(solution)/shard_map/ppermute | solution.py:545
  74.0 7.9 %collective-permute-start.1 = (f32[8,2,8,128]{3,2,1,0:T(8,128)S(1)}, f32[8,2,8,128]{3,2,1,0:T(8,128)S(1)}, u32[]{:S(2)}, u32[]{:S(2)}) collective-permute-start(f32[8,2,8,128]{3,2,1,0:T(8,128)S(1)} %get-tuple-element.21), channel_id=1, source_target_pairs={{0,7},{1,2},{2,1},{3,4},{4,3},{5,6},{6,5},{7,0},{8,15},{9,10},{10,... | collective-permute-start | bytes 196616 | tf_op jit(solution)/shard_map/ppermute | solution.py:545
  82.6 1.5 %collective-permute-start.2 = (f32[9,2,8,128]{3,2,1,0:T(8,128)S(1)}, f32[9,2,8,128]{3,2,1,0:T(8,128)S(1)}, u32[]{:S(2)}, u32[]{:S(2)}) collective-permute-start(f32[9,2,8,128]{3,2,1,0:T(8,128)S(1)} %get-tuple-element.24), channel_id=1, source_target_pairs={{0,8},{8,0},{16,24},{24,16},{32,40},{40,32},{48,56},{56,48},{64,72... | collective-permute-start | bytes 221192 | tf_op jit(solution)/shard_map/ppermute | solution.py:545
  82.7 6.1 %collective-permute-start.3 = (f32[9,2,8,128]{3,2,1,0:T(8,128)S(1)}, f32[9,2,8,128]{3,2,1,0:T(8,128)S(1)}, u32[]{:S(2)}, u32[]{:S(2)}) collective-permute-start(f32[9,2,8,128]{3,2,1,0:T(8,128)S(1)} %get-tuple-element.25), channel_id=1, source_target_pairs={{0,120},{8,16},{16,8},{24,32},{32,24},{40,48},{48,40},{56,64},{64,... | collective-permute-start | bytes 221192 | tf_op jit(solution)/shard_map/ppermute | solution.py:545
